TPU v7x, 128 devices: a whole 4x4x4 slice. The times are simulated.
128 devices in a mesh: elem: 32 (over z, y, core), grp: 4 (over x).
Axes of the slice: x: 4, y: 4, z: 4, core: 2. Of those that a mesh axis runs over, the one named last changes fastest.
Arguments:
- state: float32 [4, 72, 65536], P(None, None, ('elem', 'grp')), may hold values from -6 to 6
- surface: float32 [3, 32, 65536], P(None, None, ('elem', 'grp')), may hold values from -6 to 6
- mass: float32 [65536], P(('elem', 'grp')), may hold values from 1 to 10
- plan: int32 [2, 65536], P(None, ('elem', 'grp')), may hold values from 0 to 159, as said below
- active: int32 [65536], P(('elem', 'grp')), may hold values from 0 to 1, as said below
Outputs:
- new_state: float32 [4, 72, 65536], P(None, None, ('elem', 'grp'))
- crm_diag: float32 [3, 32, 65536], P(None, None, ('elem', 'grp'))
Inputs may be any that keep to these rules, and one draw needn't show every extreme that they name: `plan`: row 0 holds owners from 0 to 127, row 1 slots from 0 to 159. An inactive column names its own device and slot 0. Each device with active columns sends every owner the same number of them, at most 2, and one device sends exactly 2 to every owner; the active columns of all devices fill each owner's 160 slots exactly, with no slot named twice. One device has 512 // 2 active columns; every count of active columns on a device is 128 times a whole number.
All inputs are finite; a program needn't handle non-finite values.
Results may differ from a plain program's by a relative error of at most 0.0001.
Values sent between devices are 32-bit elements; how exact they have to be, the bound alone decides.
A program may use at most 128 MiB of HBM per device.

v0:
```python
import functools
import math

import jax
import jax.numpy as jnp
import ml_dtypes
import numpy as np
from jax import lax
from jax.experimental import pallas as pl
from jax.experimental.pallas import tpu as pltpu
from jax.sharding import PartitionSpec as P

LEV = 72
CZ = 58
CX = 32
EDGE = 64
LANES = 128
BLOCK = 128
ZP = 64
HALF = 2 * LEV
STATE_ROWS = 224
F32 = jnp.float32
BF16 = jnp.bfloat16
MESH = pl.DeviceIdType.MESH
UNROLL = 3


def split_np(matrix):
    high = matrix.astype(np.float32).astype(ml_dtypes.bfloat16)
    low = (matrix - high.astype(np.float64)).astype(np.float32).astype(ml_dtypes.bfloat16)
    return high, low


def tables():
    z = np.arange(CZ, dtype=np.float64)
    lev = np.arange(LEV, dtype=np.float64)
    up = np.maximum(0.0, 1.0 - np.abs(z[:, None] * ((LEV - 1) / (CZ - 1)) - lev[None, :]))
    down = np.maximum(0.0, 1.0 - np.abs(lev[:, None] * ((CZ - 1) / (LEV - 1)) - z[None, :]))
    fall = 1.0 - 0.5 * z / (CZ - 1)
    k = 0.1 + 0.2 * z / (CZ - 1)
    mix = np.zeros((CZ, CZ))
    for i in range(CZ):
        mix[i, i] += 1.0 - 2.0 * k[i]
        mix[i, min(i + 1, CZ - 1)] += k[i]
        mix[i, max(i - 1, 0)] += k[i]
    kap = mix.sum(0)
    c1 = mix @ fall
    c2 = -0.1 * (mix @ (fall * fall))
    kb = mix @ up
    qb = -0.1 * (mix @ (fall[:, None] * up))

    m = np.zeros((344, STATE_ROWS))
    p0, p1, p2 = slice(0, 72), slice(72, 144), slice(144, 216)
    m[0:CZ, p1] = kb / 0.62
    m[0:CZ, p0] = -0.3 * kb / 0.62
    m[64:64 + CZ, p2] = 0.5 * kb
    m[128:128 + CZ, p2] = qb
    dkk = down @ mix @ kb
    m[192:264, p0] = dkk / 1.24 - down @ up
    m[192:264, p1] = 0.8 * dkk / 1.24
    m[264:336, p0] = 0.3 * dkk / 1.24
    m[264:336, p1] = 0.3 * 0.8 * dkk / 1.24 - down @ up
    m[336, p2] = (kap * c1) @ (0.5 * kb)
    m[337, p2] = (kap * c2) @ (0.5 * kb)
    m[338, p2] = (kap * c1) @ qb
    m[339, p2] = (kap * c2) @ qb
    m[340, p2] = kap @ qb
    m[341, p0] = kap @ kb
    m[341, p1] = 0.8 * (kap @ kb)
    m[342, p0] = up.sum(0)
    hi, lo = split_np(m)
    maps = np.concatenate([hi, lo, hi], 1)
    maps = np.concatenate([maps, np.zeros((8, maps.shape[1]), maps.dtype)], 0)

    t = np.zeros((HALF, 2 * ZP))
    t[0:72, 0:CZ] = down @ mix / 1.24
    t[72:144, 0:CZ] = 0.3 * (down @ mix) / 1.24
    t[0:72, ZP:ZP + CZ] = -0.8 * down / 1.24
    t[72:144, ZP:ZP + CZ] = down / 1.24
    hi, lo = split_np(t)
    tail = np.concatenate([hi, lo, hi], 1)

    e = np.zeros((HALF, HALF))
    e[0:72, 0:72] = down @ (mix @ kb - up)
    e[72:144, 72:144] = e[0:72, 0:72]
    hi, lo = split_np(e)
    passive = np.concatenate([hi, lo, hi], 1)
    drift = np.repeat(((down @ (mix @ (mix @ fall))) / CX)[:, None], LANES, 1).astype(np.float32)

    levels = np.zeros((5, ZP))
    levels[0, :CZ] = c1
    levels[1, :CZ] = c2
    levels[2, :CZ] = 0.124 * (1.0 - 2.0 * k)
    levels[3, :CZ] = 0.124 * k
    levels[4, :CZ] = kap
    levels = np.repeat(levels.reshape(-1)[:, None], LANES, 1).astype(np.float32)
    sums = (float((kap * c1 * c1).sum()), float((kap * c1 * c2).sum()), float((kap * c2 * c2).sum()),
            float((kap * c1).sum()), float((kap * c2).sum()))
    return maps, tail, passive, drift, levels, sums


def halves(x):
    high = x.astype(BF16)
    return high, (x - high.astype(F32)).astype(BF16)


def dot(a, b):
    return lax.dot_general(a, b, (((1,), (0,)), ((), ())), preferred_element_type=F32)


def dot_t(a, b):
    return lax.dot_general(a, b, (((1,), (1,)), ((), ())), preferred_element_type=F32)


def east(f):
    return jnp.concatenate([f[1:], pltpu.roll(f[0], 7, 0)[None]], 0)


def west(f):
    return jnp.concatenate([pltpu.roll(f[3], 1, 0)[None], f[:3]], 0)


def xsum(f):
    return jnp.sum((f[0] + f[1]) + (f[2] + f[3]), axis=0, keepdims=True)


def cloud(sums, g_hi, g_lo, maps_ref, tail_ref, lev_ref, sur_ref, prof_ref, part_ref, diag_ref):
    s11, s12, s22, sc1, sc2 = sums
    prof_ref[...] = dot(maps_ref[...], jnp.concatenate([g_hi, g_hi, g_lo], 0))

    def rows(j):
        return jnp.stack([sur_ref[pl.ds(CX * j + v, 8, stride=4), :] for v in range(4)], 0)

    r0, r1, s2 = rows(0), rows(1), rows(2)
    sy = (r1 - 0.3 * r0) * (1.0 / 0.62)
    sw = r0 + 0.8 * r1

    def parts(s):
        e, w = east(s), west(s)
        return 0.6 * s + 0.2 * (e + w), e - w

    ay, dy = parts(sy)
    a2, d2 = parts(s2)
    af, df = 0.5 * a2, 0.5 * d2

    def level(ref, base, z):
        return ref[pl.ds(base + z, 1), :][None]

    def horizontal(z):
        c1 = level(lev_ref, 0, z)
        turn = level(prof_ref, 128, z) + level(lev_ref, ZP, z) * s2
        y = (level(prof_ref, 0, z) + c1 * ay) + turn * dy
        f2 = (level(prof_ref, 64, z) + c1 * af) + turn * df
        one = jnp.log(1.0 + jnp.exp2(y * (0.62 * math.log2(math.e))))
        y = y - one
        e, w = east(y), west(y)
        return (3.0 * y + (e + w)) - f2 * (e - w), one

    def vertical(z, h, above, below):
        v = level(lev_ref, 2 * ZP, z) * h + level(lev_ref, 3 * ZP, z) * (above + below)
        two = jnp.maximum(jnp.log(1.0 + jnp.exp(jnp.minimum(v, 80.0))), v)
        vs = (v[0] + v[1]) + (v[2] + v[3])
        ts = (two[0] + two[1]) + (two[2] + two[3])
        part_ref[pl.ds(pl.multiple_of(z * 8, 8), 8), :] = vs - 0.62 * ts
        return v, two

    h0, rain = horizontal(0)

    def step(i, carry):
        h, below, rain, total_v, total_2 = carry
        for u in range(UNROLL):
            z = 1 + i * UNROLL + u
            above, one = horizontal(z)
            v, two = vertical(z - 1, h, above, below)
            rain, total_v, total_2 = rain + one, total_v + v, total_2 + two
            h, below = above, h
        return h, below, rain, total_v, total_2

    zero = jnp.zeros_like(rain)
    carry = lax.fori_loop(0, (CZ - 1) // UNROLL, step, (h0, h0, rain, zero, zero))
    h, below, rain, total_v, total_2 = carry
    v, two = vertical(CZ - 1, h, h, below)
    total_v, total_2 = total_v + v, total_2 + two
    sum_y = total_v - 0.62 * total_2

    aw, dw = parts(sw)
    ew, ef = s2 * dw, s2 * df
    haw, hdw, hew = east(aw) - west(aw), east(dw) - west(dw), east(ew) - west(ew)
    g11 = xsum(af * haw)
    g12 = xsum(af * hdw + df * haw)
    g13 = xsum(af * hew + ef * haw)
    g22 = xsum(df * hdw)
    g23 = xsum(df * hew + ef * hdw)
    g33 = xsum(ef * hew)
    c1 = lev_ref[0:ZP, :]
    c2 = lev_ref[ZP:2 * ZP, :]
    kap = lev_ref[4 * ZP:5 * ZP, :]
    pf = prof_ref[64:128, :]
    q = prof_ref[128:192, :]
    gram = c1 * (c1 * g11 + q * g12 + c2 * g13) + q * (q * g22 + c2 * g23) + (c2 * c2) * g33
    mean_w = c1 * (xsum(sw) * (1.0 / CX)) + c2 * (xsum(ew) * (1.0 / CX)) - (0.2 / CX) * gram
    qk = q * kap
    sqp = jnp.sum(qk * pf, axis=0, keepdims=True)
    sqq = jnp.sum(qk * q, axis=0, keepdims=True)
    s1p, s2p, s1q, sq2, sq, spw, sb = [prof_ref[336 + i:337 + i, :] for i in range(7)]
    w1 = (spw + sc1 * aw) + (sq * dw + sc2 * ew)
    sum_w = (
        (0.6 * w1 + 0.2 * (east(w1) + west(w1)))
        - 0.2 * (
            haw * ((s1p + s11 * af) + (s1q * df + s12 * ef))
            + hdw * ((sqp + s1q * af) + (sqq * df + sq2 * ef))
            + hew * ((s2p + s12 * af) + (sq2 * df + s22 * ef))
        )
    )
    rain = 0.5 * (rain + total_2)
    moist = (sum_y + 0.3 * sum_w) * (1.0 / (1.24 * CZ))
    heat = (sum_w - 0.8 * sum_y) * (1.0 / (1.24 * CZ)) - sb * (1.0 / CZ)
    for i, rows_out in enumerate((rain, moist, heat)):
        for v in range(4):
            diag_ref[pl.ds(CX * i + v, 8, stride=4), :] = rows_out[v]

    mean_y = part_ref[pl.ds(0, ZP, stride=8), :]
    for s in range(1, 8):
        mean_y = mean_y + part_ref[pl.ds(s, ZP, stride=8), :]
    live = lax.broadcasted_iota(jnp.int32, (ZP, BLOCK), 0) < CZ
    mean_y = jnp.where(live, mean_y * (1.0 / CX), 0.0)
    hi, lo = halves(jnp.concatenate([mean_w, mean_y], 0))
    return prof_ref[192:336, :] + dot(tail_ref[...], jnp.concatenate([hi, hi, lo], 0))


def kernel(sums, n_elem, state_ref, surface_ref, mass_ref, active_ref, maps_ref, tail_ref, passive_ref,
           drift_ref, lev_ref, out_ref, diag_out_ref,
           xs, hi_ref, lo_ref, su, ones_ref, send, recv, sur, prof, part, diag, both_hi, both_lo,
           in_sem, send_sem, recv_sem):
    e, g = lax.axis_index("elem"), lax.axis_index("grp")
    after = lax.rem(e + 1, n_elem)
    before = lax.rem(e + n_elem - 1, n_elem)
    barrier = pltpu.get_barrier_semaphore()
    for other in (before, after):
        pl.semaphore_signal(barrier, inc=1, device_id=(other, g), device_id_type=MESH)

    loads = [
        pltpu.make_async_copy(state_ref.at[:, pl.ds(a, n)], xs.at[:, pl.ds(a, n)], in_sem.at[i])
        for i, (a, n) in enumerate(((0, LANES), (3 * LANES, LANES), (LANES, 2 * LANES)))
    ] + [pltpu.make_async_copy(surface_ref, su, in_sem.at[3])]
    for load in loads:
        load.start()

    lane = lax.broadcasted_iota(jnp.int32, (1, LANES), 1)
    low = lane < EDGE

    act = [active_ref[:, pl.ds(LANES * b, LANES)].astype(F32) for b in range(4)]
    nil = jnp.zeros((1, LANES), F32)
    inner = [jnp.where(low, 0.0, act[0]), act[1], act[2], jnp.where(low, act[3], 0.0)]
    outer = [jnp.where(low, act[0], 0.0), nil, nil, jnp.where(low, 0.0, act[3])]
    marks = jnp.concatenate(inner + outer, 0)
    r = lax.broadcasted_iota(jnp.int32, (LANES, LANES), 0)
    c = lax.broadcasted_iota(jnp.int32, (LANES, LANES), 1)
    tri = jnp.where(r <= c, 1.0, 0.0).astype(BF16)
    counts = dot(marks.astype(BF16), jnp.concatenate([tri, jnp.ones((LANES, LANES), BF16)], 1))
    run, tot = counts[:, :LANES], counts[:, LANES:]
    offset = nil
    place = []
    for b in range(4):
        inside = run[b:b + 1] + (offset - 1.0)
        outside = (2.0 * BLOCK) - (run[4 + b:5 + b] + (tot[4:5] if b == 3 else 0.0))
        spot = inside if b in (1, 2) else jnp.where(low if b == 3 else ~low, inside, outside)
        place.append(jnp.where(act[b] > 0.5, spot, -1.0))
        offset = offset + tot[b:b + 1]
    where = lax.broadcasted_iota(jnp.int32, (2 * BLOCK, LANES), 0).astype(F32)
    for b in range(4):
        ones_ref[:, LANES * b:LANES * (b + 1)] = jnp.where(where == place[b], 1.0, 0.0).astype(BF16)

    mass0 = mass_ref[:, 0:LANES]
    mass3 = mass_ref[:, 3 * LANES:4 * LANES]
    loads[0].wait()
    loads[1].wait()
    first, last = xs[:, 0:LANES], xs[:, 3 * LANES:4 * LANES]
    send[0, 0:HALF, :] = jnp.where(low, first[:HALF], pltpu.roll(first[HALF:], EDGE, 1))
    send[1, 0:HALF, :] = jnp.where(low, pltpu.roll(last[:HALF], EDGE, 1), last[HALF:])
    send[0, HALF:, :] = jnp.broadcast_to(pltpu.roll(mass0, EDGE, 1), (8, LANES))
    send[1, HALF:, :] = jnp.broadcast_to(pltpu.roll(mass3, EDGE, 1), (8, LANES))
    pl.semaphore_wait(barrier, 2)
    copies = [
        pltpu.make_async_remote_copy(
            src_ref=send.at[i], dst_ref=recv.at[i], send_sem=send_sem.at[i], recv_sem=recv_sem.at[i],
            device_id=(other, g), device_id_type=MESH)
        for i, other in enumerate((before, after))
    ]
    for copy in copies:
        copy.start()

    loads[2].wait()
    loads[3].wait()

    def split_state(lanes):
        hi, lo = halves(xs[:, lanes])
        hi_ref[0:288, lanes] = hi
        lo_ref[0:288, lanes] = lo

    split_state(slice(0, 4 * LANES))
    hi, lo = halves(su[...])
    hi_ref[288:384, :] = hi
    lo_ref[288:384, :] = lo

    def block(i):
        pick = ones_ref[BLOCK * i:BLOCK * (i + 1), :]
        g_hi = dot_t(hi_ref[0:STATE_ROWS, :], pick).astype(BF16)
        g_lo = dot_t(lo_ref[0:STATE_ROWS, :], pick).astype(BF16)
        sur[...] = dot_t(hi_ref[288:384, :], pick) + dot_t(lo_ref[288:384, :], pick)
        tend = cloud(sums, g_hi, g_lo, maps_ref, tail_ref, lev_ref, sur, prof, part, diag)
        hi, lo = halves(jnp.concatenate([tend, diag[...]], 0))
        both_hi[:, BLOCK * i:BLOCK * (i + 1)] = hi
        both_lo[:, BLOCK * i:BLOCK * (i + 1)] = lo

    block(0)

    for copy in copies:
        copy.wait()
    for lanes, own, own_mass, other, keep in (
        (slice(0, LANES), low, mass0, 1, True), (slice(3 * LANES, 4 * LANES), ~low, mass3, 0, False)):
        other_mass = recv[other, HALF:HALF + 1, :]
        share = jnp.where(own, own_mass / (own_mass + other_mass), 1.0)
        rest = jnp.where(own, other_mass / (own_mass + other_mass), 0.0)
        got = recv[other, 0:HALF, :]
        moved = pltpu.roll(got, EDGE, 1)
        top, bottom = (got, moved) if keep else (moved, got)
        xs[0:HALF, lanes] = xs[0:HALF, lanes] * share + top * rest
        xs[HALF:, lanes] = xs[HALF:, lanes] * share + bottom * rest
        split_state(lanes)

    block(1)

    full_hi, full_lo = hi_ref[HALF:2 * HALF, :], lo_ref[HALF:2 * HALF, :]
    slow = dot(passive_ref[...], jnp.concatenate([full_hi, full_hi, full_lo], 0))
    for b in range(4):
        lanes = slice(LANES * b, LANES * (b + 1))
        mean2 = jnp.sum(su[2 * CX:3 * CX, lanes], axis=0, keepdims=True)
        on = act[b] > 0.5
        out_ref[HALF:HALF + LEV, lanes] = xs[HALF:HALF + LEV, lanes] + jnp.where(
            on, slow[:LEV, lanes] + drift_ref[...] * mean2, 0.0)
        out_ref[HALF + LEV:, lanes] = xs[HALF + LEV:, lanes] + jnp.where(on, slow[LEV:, lanes], 0.0)

    back = dot(both_hi[...], ones_ref[...]) + dot(both_lo[...], ones_ref[...])
    out_ref[0:HALF, :] = xs[0:HALF, :] + back[0:HALF]
    diag_out_ref[...] = back[HALF:]


def body(n_elem, state, surface, mass, plan, active):
    cols = state.shape[2]
    maps, tail, passive, drift, levels, sums = tables()
    any_space = pl.BlockSpec(memory_space=pl.ANY)
    vmem = pl.BlockSpec(memory_space=pltpu.VMEM)
    new_state, diag = pl.pallas_call(
        functools.partial(kernel, sums, n_elem),
        out_shape=(jax.ShapeDtypeStruct((4 * LEV, cols), F32), jax.ShapeDtypeStruct((3 * CX, cols), F32)),
        in_specs=[any_space, any_space] + [vmem] * 7,
        out_specs=(vmem, vmem),
        scratch_shapes=[
            pltpu.VMEM((4 * LEV, cols), F32),
            pltpu.VMEM((384, cols), BF16),
            pltpu.VMEM((384, cols), BF16),
            pltpu.VMEM((3 * CX, cols), F32),
            pltpu.VMEM((2 * BLOCK, cols), BF16),
            pltpu.VMEM((2, HALF + 8, LANES), F32),
            pltpu.VMEM((2, HALF + 8, LANES), F32),
            pltpu.VMEM((3 * CX, BLOCK), F32),
            pltpu.VMEM((352, BLOCK), F32),
            pltpu.VMEM((ZP * 8, BLOCK), F32),
            pltpu.VMEM((3 * CX, BLOCK), F32),
            pltpu.VMEM((HALF + 3 * CX, 2 * BLOCK), BF16),
            pltpu.VMEM((HALF + 3 * CX, 2 * BLOCK), BF16),
            pltpu.SemaphoreType.DMA((4,)),
            pltpu.SemaphoreType.DMA((2,)),
            pltpu.SemaphoreType.DMA((2,)),
        ],
        compiler_params=pltpu.CompilerParams(
            collective_id=0, has_side_effects=True, vmem_limit_bytes=32 * 1024 * 1024),
    )(
        state.reshape(4 * LEV, cols), surface.reshape(3 * CX, cols), mass.reshape(1, cols),
        active.reshape(1, cols), maps, tail, passive, drift, levels,
    )
    return new_state.reshape(state.shape), diag.reshape(surface.shape)


def solution(mesh):
    both = ("elem", "grp")
    return jax.shard_map(
        functools.partial(body, mesh.shape["elem"]),
        mesh=mesh,
        in_specs=(P(None, None, both), P(None, None, both), P(both), P(None, both), P(both)),
        out_specs=(P(None, None, both), P(None, None, both)),
        check_vma=False,
    )
```

profile of v0, /device:TPU:0, one launch (start us, length us, event | category | flops | bytes accessed | tf_op | source)
XLA Modules:
  0.0 21.6 jit_solution(18102184961649889418)
XLA Ops:
  0.6 0.0 copy-start.8
  0.6 0.0 copy-start.7
  0.7 0.7 %copy-done.8 = s32[512]{0:T(512)S(1)} copy-done((s32[512]{0:T(512)S(1)}, s32[512]{0:T(512)}, u32[]{:S(2)}) %copy-start.8) | copy-done | bytes 2072
  1.3 0.0 copy-done.7
  1.3 0.0 copy-start
  1.3 1.1 %copy-done = f32[4,72,512]{2,1,0:T(8,128)S(1)} copy-done((f32[4,72,512]{2,1,0:T(8,128)S(1)}, f32[4,72,512]{2,1,0:T(8,128)}, u32[]{:S(2)}) %copy-start) | copy-done | bytes 589848
  2.4 0.0 copy-start.1
  2.4 1.0 %copy-done.1 = bf16[352,672]{1,0:T(8,128)(2,1)S(1)} copy-done((bf16[352,672]{1,0:T(8,128)(2,1)S(1)}, bf16[352,672]{1,0:T(8,128)(2,1)}, u32[]{:S(2)}) %copy-start.1) | copy-done | bytes 473112
  3.4 0.0 copy-start.2
  3.4 0.9 %copy-done.2 = f32[3,32,512]{2,1,0:T(8,128)S(1)} copy-done((f32[3,32,512]{2,1,0:T(8,128)S(1)}, f32[3,32,512]{2,1,0:T(8,128)}, u32[]{:S(2)}) %copy-start.2) | copy-done | bytes 196632
  4.4 0.0 copy-start.3
  4.4 0.9 %copy-done.3 = f32[320,128]{1,0:T(8,128)S(1)} copy-done((f32[320,128]{1,0:T(8,128)S(1)}, f32[320,128]{1,0:T(8,128)}, u32[]{:S(2)}) %copy-start.3) | copy-done | bytes 163864
  5.3 0.0 copy-start.4
  5.3 0.9 %copy-done.4 = bf16[144,432]{1,0:T(8,128)(2,1)S(1)} copy-done((bf16[144,432]{1,0:T(8,128)(2,1)S(1)}, bf16[144,432]{1,0:T(8,128)(2,1)}, u32[]{:S(2)}) %copy-start.4) | copy-done | bytes 124440
  6.2 0.0 copy-start.5
  6.2 0.9 %copy-done.5 = bf16[144,384]{1,0:T(8,128)(2,1)S(1)} copy-done((bf16[144,384]{1,0:T(8,128)(2,1)S(1)}, bf16[144,384]{1,0:T(8,128)(2,1)}, u32[]{:S(2)}) %copy-start.5) | copy-done | bytes 110616
  7.1 0.0 copy-start.6
  7.1 0.8 %copy-done.6 = f32[72,128]{1,0:T(8,128)S(1)} copy-done((f32[72,128]{1,0:T(8,128)S(1)}, f32[72,128]{1,0:T(8,128)}, u32[]{:S(2)}) %copy-start.6) | copy-done | bytes 36888
  7.9 12.2 %shard_map.104 = (f32[288,512]{1,0:T(8,128)S(1)}, f32[96,512]{1,0:T(8,128)S(1)}) custom-call(f32[288,512]{1,0:T(8,128)S(1)} %bitcast.6, f32[96,512]{1,0:T(8,128)S(1)} %bitcast.8, f32[1,512]{1,0:T(1,128)S(1)} %bitcast.10, s32[1,512]{1,0:T(1,128)S(1)} %bitcast.11, bf16[352,672]{1,0:T(8,128)(2,1)S(1)} %copy-done.1, bf16[144,384]{1,0:T(8,128)(2,1)S(1)} %copy-done.5, ...), custom_call_target="tpu_custom_call" | custom-call | tf_op jit(solution)/shard_map/pallas_call | solution.py:354
  20.1 0.8 %copy.13 = f32[4,72,512]{2,1,0:T(8,128)} copy(f32[4,72,512]{2,1,0:T(8,128)S(1)} %bitcast.7) | data formatting | bytes 1179648
  20.9 0.7 %copy.14 = f32[3,32,512]{2,1,0:T(8,128)} copy(f32[3,32,512]{2,1,0:T(8,128)S(1)} %bitcast.9) | data formatting | bytes 393216
Async XLA Ops:
  0.6 0.7 %copy-start.8 = (s32[512]{0:T(512)S(1)}, s32[512]{0:T(512)}, u32[]{:S(2)}) copy-start(s32[512]{0:T(512)} %param.13) | copy-start | bytes 6148
  0.6 0.7 %copy-start.7 = (f32[512]{0:T(512)S(1)}, f32[512]{0:T(512)}, u32[]{:S(2)}) copy-start(f32[512]{0:T(512)} %param.12) | copy-start | bytes 6148
  1.3 1.1 %copy-start = (f32[4,72,512]{2,1,0:T(8,128)S(1)}, f32[4,72,512]{2,1,0:T(8,128)}, u32[]{:S(2)}) copy-start(f32[4,72,512]{2,1,0:T(8,128)} %param.10) | copy-start | bytes 1769476
  2.4 1.0 %copy-start.1 = (bf16[352,672]{1,0:T(8,128)(2,1)S(1)}, bf16[352,672]{1,0:T(8,128)(2,1)}, u32[]{:S(2)}) copy-start(bf16[352,672]{1,0:T(8,128)(2,1)} %constant.10.clone.maps_ref) | copy-start | bytes 1419268
  3.4 0.9 %copy-start.2 = (f32[3,32,512]{2,1,0:T(8,128)S(1)}, f32[3,32,512]{2,1,0:T(8,128)}, u32[]{:S(2)}) copy-start(f32[3,32,512]{2,1,0:T(8,128)} %param.11) | copy-start | bytes 589828
  4.4 0.9 %copy-start.3 = (f32[320,128]{1,0:T(8,128)S(1)}, f32[320,128]{1,0:T(8,128)}, u32[]{:S(2)}) copy-start(f32[320,128]{1,0:T(8,128)} %constant.14.clone.lev_ref) | copy-start | bytes 491524
  5.3 0.9 %copy-start.4 = (bf16[144,432]{1,0:T(8,128)(2,1)S(1)}, bf16[144,432]{1,0:T(8,128)(2,1)}, u32[]{:S(2)}) copy-start(bf16[144,432]{1,0:T(8,128)(2,1)} %constant.12.clone.passive_ref) | copy-start | bytes 373252
  6.2 0.9 %copy-start.5 = (bf16[144,384]{1,0:T(8,128)(2,1)S(1)}, bf16[144,384]{1,0:T(8,128)(2,1)}, u32[]{:S(2)}) copy-start(bf16[144,384]{1,0:T(8,128)(2,1)} %constant.11.clone.tail_ref) | copy-start | bytes 331780
  7.1 0.8 %copy-start.6 = (f32[72,128]{1,0:T(8,128)S(1)}, f32[72,128]{1,0:T(8,128)}, u32[]{:S(2)}) copy-start(f32[72,128]{1,0:T(8,128)} %constant.13.clone.drift_ref) | copy-start | bytes 110596
where the time goes:
time: 22 us; the launch traced here: 21.6 us
  Pallas kernels  12.2 us (55%)
  local copies, waits for them, and re-layouts  8.7 us (40%)
  between operations  0.66 us (3%)
    pallas_call x1, Pallas kernels, body(): pl.pallas_call(functools.partial(kernel, sums, n_elem), out_shape=(jax.Sh...  12.2 us
    unnamed x20, local copies, waits for them, and re-layouts  8.7 us

commit v1 on v0

--- a/solution.py
+++ b/solution.py
@@ -22,7 +22,7 @@
 F32 = jnp.float32
 BF16 = jnp.bfloat16
 MESH = pl.DeviceIdType.MESH
-UNROLL = 3
+UNROLL = 19
 
 
 def split_np(matrix):
@@ -228,9 +228,10 @@
     return prof_ref[192:336, :] + dot(tail_ref[...], jnp.concatenate([hi, hi, lo], 0))
 
 
-def kernel(sums, n_elem, state_ref, surface_ref, mass_ref, active_ref, maps_ref, tail_ref, passive_ref,
-           drift_ref, lev_ref, out_ref, diag_out_ref,
+def kernel(sums, n_elem, state_ref, surface_ref, mass_hbm, active_hbm, maps_hbm, tail_hbm, passive_hbm,
+           drift_hbm, lev_hbm, out_ref, diag_out_ref,
            xs, hi_ref, lo_ref, su, ones_ref, send, recv, sur, prof, part, diag, both_hi, both_lo,
+           mass_ref, active_ref, maps_ref, tail_ref, passive_ref, drift_ref, lev_ref,
            in_sem, send_sem, recv_sem):
     e, g = lax.axis_index("elem"), lax.axis_index("grp")
     after = lax.rem(e + 1, n_elem)
@@ -243,8 +244,15 @@
         pltpu.make_async_copy(state_ref.at[:, pl.ds(a, n)], xs.at[:, pl.ds(a, n)], in_sem.at[i])
         for i, (a, n) in enumerate(((0, LANES), (3 * LANES, LANES), (LANES, 2 * LANES)))
     ] + [pltpu.make_async_copy(surface_ref, su, in_sem.at[3])]
-    for load in loads:
+    small = [
+        pltpu.make_async_copy(a, b, in_sem.at[4 + i])
+        for i, (a, b) in enumerate((
+            (mass_hbm, mass_ref), (active_hbm, active_ref), (maps_hbm, maps_ref), (lev_hbm, lev_ref),
+            (tail_hbm, tail_ref), (passive_hbm, passive_ref), (drift_hbm, drift_ref)))
+    ]
+    for load in loads[:2] + small[:2] + loads[2:] + small[2:]:
         load.start()
+    small[1].wait()
 
     lane = lax.broadcasted_iota(jnp.int32, (1, LANES), 1)
     low = lane < EDGE
@@ -271,6 +279,7 @@
     for b in range(4):
         ones_ref[:, LANES * b:LANES * (b + 1)] = jnp.where(where == place[b], 1.0, 0.0).astype(BF16)
 
+    small[0].wait()
     mass0 = mass_ref[:, 0:LANES]
     mass3 = mass_ref[:, 3 * LANES:4 * LANES]
     loads[0].wait()
@@ -303,6 +312,9 @@
     hi_ref[288:384, :] = hi
     lo_ref[288:384, :] = lo
 
+    for load in small[2:]:
+        load.wait()
+
     def block(i):
         pick = ones_ref[BLOCK * i:BLOCK * (i + 1), :]
         g_hi = dot_t(hi_ref[0:STATE_ROWS, :], pick).astype(BF16)
@@ -346,15 +358,28 @@
     diag_out_ref[...] = back[HALF:]
 
 
+def write(state_ref, diag_ref, state_out, diag_out, sem):
+    copies = [pltpu.make_async_copy(state_ref, state_out, sem.at[0]),
+              pltpu.make_async_copy(diag_ref, diag_out, sem.at[1])]
+    for copy in copies:
+        copy.start()
+    for copy in copies:
+        copy.wait()
+
+
 def body(n_elem, state, surface, mass, plan, active):
     cols = state.shape[2]
     maps, tail, passive, drift, levels, sums = tables()
-    any_space = pl.BlockSpec(memory_space=pl.ANY)
+    hbm = pl.BlockSpec(memory_space=pltpu.HBM)
     vmem = pl.BlockSpec(memory_space=pltpu.VMEM)
+    state, surface, mass, active, maps, tail, passive, drift, levels = [
+        pltpu.with_memory_space_constraint(x, pltpu.HBM) for x in (
+            state.reshape(4 * LEV, cols), surface.reshape(3 * CX, cols), mass.reshape(1, cols),
+            active.reshape(1, cols), *map(jnp.asarray, (maps, tail, passive, drift, levels)))]
     new_state, diag = pl.pallas_call(
         functools.partial(kernel, sums, n_elem),
-        out_shape=(jax.ShapeDtypeStruct((4 * LEV, cols), F32), jax.ShapeDtypeStruct((3 * CX, cols), F32)),
-        in_specs=[any_space, any_space] + [vmem] * 7,
+        out_shape=(pltpu.VMEM((4 * LEV, cols), F32), pltpu.VMEM((3 * CX, cols), F32)),
+        in_specs=[hbm] * 9,
         out_specs=(vmem, vmem),
         scratch_shapes=[
             pltpu.VMEM((4 * LEV, cols), F32),
@@ -370,17 +395,30 @@
             pltpu.VMEM((3 * CX, BLOCK), F32),
             pltpu.VMEM((HALF + 3 * CX, 2 * BLOCK), BF16),
             pltpu.VMEM((HALF + 3 * CX, 2 * BLOCK), BF16),
-            pltpu.SemaphoreType.DMA((4,)),
+            pltpu.VMEM((1, cols), F32),
+            pltpu.VMEM((1, cols), jnp.int32),
+            pltpu.VMEM(maps.shape, BF16),
+            pltpu.VMEM(tail.shape, BF16),
+            pltpu.VMEM(passive.shape, BF16),
+            pltpu.VMEM(drift.shape, F32),
+            pltpu.VMEM(levels.shape, F32),
+            pltpu.SemaphoreType.DMA((11,)),
             pltpu.SemaphoreType.DMA((2,)),
             pltpu.SemaphoreType.DMA((2,)),
         ],
         compiler_params=pltpu.CompilerParams(
             collective_id=0, has_side_effects=True, vmem_limit_bytes=32 * 1024 * 1024),
     )(
-        state.reshape(4 * LEV, cols), surface.reshape(3 * CX, cols), mass.reshape(1, cols),
-        active.reshape(1, cols), maps, tail, passive, drift, levels,
+        state, surface, mass, active, maps, tail, passive, drift, levels,
     )
-    return new_state.reshape(state.shape), diag.reshape(surface.shape)
+    new_state, diag = pl.pallas_call(
+        write,
+        out_shape=(jax.ShapeDtypeStruct(new_state.shape, F32), jax.ShapeDtypeStruct(diag.shape, F32)),
+        in_specs=[vmem, vmem],
+        out_specs=(hbm, hbm),
+        scratch_shapes=[pltpu.SemaphoreType.DMA((2,))],
+    )(pltpu.with_memory_space_constraint(new_state, pltpu.VMEM), pltpu.with_memory_space_constraint(diag, pltpu.VMEM))
+    return new_state.reshape(4, LEV, cols), diag.reshape(3, CX, cols)
 
 
 def solution(mesh):

time: 22 us -> 13.8 us (0.63); the launches traced: 21.6 us -> 13.7 us
  local copies, waits for them, and re-layouts: 8.7 us -> 0 us
  Pallas kernels: 12.2 us -> 13 us
    unnamed x20 -> x0, local copies, waits for them, and re-layouts: 8.7 us -> none
    pallas_call x1 -> x2, Pallas kernels: 12.2 us -> 13 us  [the longest x1 12.1 us: body(): pl.pallas_call(functools.partial(kernel, sums, n_elem), out_shape=(pltpu....]
where the time goes in v1:
time: 13.8 us; the launch traced here: 13.7 us
  Pallas kernels  13 us (94%)
  between operations  0.64 us (5%)
    pallas_call x1, Pallas kernels, body(): pl.pallas_call(functools.partial(kernel, sums, n_elem), out_shape=(pltpu....  12.1 us
    pallas_call x1, Pallas kernels, body(): pl.pallas_call(write, out_shape=(jax.ShapeDtypeStruct(new_state.shape, F3...  0.89 us

profile of v1, /device:TPU:0, one launch (start us, length us, event | category | flops | bytes accessed | tf_op | source)
XLA Modules:
  0.0 13.7 jit_solution(9256908273670056814)
XLA Ops:
  0.6 12.1 %shard_map.104 = (f32[288,512]{1,0:T(8,128)S(1)}, f32[96,512]{1,0:T(8,128)S(1)}) custom-call(f32[288,512]{1,0:T(8,128)} %bitcast.6, f32[96,512]{1,0:T(8,128)} %bitcast.7, f32[1,512]{1,0:T(1,128)} %bitcast.8, s32[1,512]{1,0:T(1,128)} %bitcast.9, bf16[352,672]{1,0:T(8,128)(2,1)} %constant.10.clone.maps_hbm, bf16[144,384]{1,0:T(8,128)(2,1)} %constant.11.clone.tail_hbm, ...), custom_call_target="tpu_custom_call" | custom-call | tf_op jit(solution)/shard_map/pallas_call | solution.py:379
  12.8 0.9 %shard_map.105 = (f32[288,512]{1,0:T(8,128)}, f32[96,512]{1,0:T(8,128)}) custom-call(f32[288,512]{1,0:T(8,128)S(1)} %get-tuple-element.6.state_ref, f32[96,512]{1,0:T(8,128)S(1)} %get-tuple-element.7.diag_ref), custom_call_target="tpu_custom_call" | custom-call | tf_op jit(solution)/shard_map/pallas_call | solution.py:414

commit v2 on v1

v2 whole, which is shorter than its diff:
```python
import functools
import math

import jax
import jax.numpy as jnp
import ml_dtypes
import numpy as np
from jax import lax
from jax.experimental import pallas as pl
from jax.experimental.pallas import tpu as pltpu
from jax.sharding import PartitionSpec as P

LEV = 72
CZ = 58
CX = 32
EDGE = 64
LANES = 128
BLOCK = 128
ZP = 64
HALF = 2 * LEV
STATE_ROWS = 224
F32 = jnp.float32
BF16 = jnp.bfloat16
MESH = pl.DeviceIdType.MESH


def split_np(matrix):
    high = matrix.astype(np.float32).astype(ml_dtypes.bfloat16)
    low = (matrix - high.astype(np.float64)).astype(np.float32).astype(ml_dtypes.bfloat16)
    return high, low


def tables():
    z = np.arange(CZ, dtype=np.float64)
    lev = np.arange(LEV, dtype=np.float64)
    up = np.maximum(0.0, 1.0 - np.abs(z[:, None] * ((LEV - 1) / (CZ - 1)) - lev[None, :]))
    down = np.maximum(0.0, 1.0 - np.abs(lev[:, None] * ((CZ - 1) / (LEV - 1)) - z[None, :]))
    fall = 1.0 - 0.5 * z / (CZ - 1)
    k = 0.1 + 0.2 * z / (CZ - 1)
    mix = np.zeros((CZ, CZ))
    for i in range(CZ):
        mix[i, i] += 1.0 - 2.0 * k[i]
        mix[i, min(i + 1, CZ - 1)] += k[i]
        mix[i, max(i - 1, 0)] += k[i]
    kap = mix.sum(0)
    c1 = mix @ fall
    c2 = -0.1 * (mix @ (fall * fall))
    kb = mix @ up
    qb = -0.1 * (mix @ (fall[:, None] * up))

    m = np.zeros((344, STATE_ROWS))
    p0, p1, p2 = slice(0, 72), slice(72, 144), slice(144, 216)
    m[0:CZ, p1] = kb / 0.62
    m[0:CZ, p0] = -0.3 * kb / 0.62
    m[64:64 + CZ, p2] = -0.25 * kb
    m[128:128 + CZ, p2] = qb
    dkk = down @ mix @ kb
    m[192:264, p0] = dkk / 1.24 - down @ up
    m[192:264, p1] = 0.8 * dkk / 1.24
    m[264:336, p0] = 0.3 * dkk / 1.24
    m[264:336, p1] = 0.3 * 0.8 * dkk / 1.24 - down @ up
    m[336, p2] = (kap * c1) @ (-0.25 * kb)
    m[337, p2] = (kap * c2) @ (-0.25 * kb)
    m[338, p2] = (kap * c1) @ qb
    m[339, p2] = (kap * c2) @ qb
    m[340, p2] = kap @ qb
    m[341, p0] = kap @ kb
    m[341, p1] = 0.8 * (kap @ kb)
    m[342, p0] = up.sum(0)
    hi, lo = split_np(m)
    maps = np.concatenate([hi, lo, hi], 1)
    maps = np.concatenate([maps, np.zeros((8, maps.shape[1]), maps.dtype)], 0)

    t = np.zeros((HALF, 2 * ZP))
    t[0:72, 0:CZ] = down @ mix / 1.24
    t[72:144, 0:CZ] = 0.3 * (down @ mix) / 1.24
    t[0:72, ZP:ZP + CZ] = -0.8 * down / 1.24
    t[72:144, ZP:ZP + CZ] = down / 1.24
    hi, lo = split_np(t)
    tail = np.concatenate([hi, lo, hi], 1)

    e = np.zeros((HALF, HALF))
    e[0:72, 0:72] = down @ (mix @ kb - up)
    e[72:144, 72:144] = e[0:72, 0:72]
    hi, lo = split_np(e)
    passive = np.concatenate([hi, lo, hi], 1)
    drift = np.repeat(((down @ (mix @ (mix @ fall))) / CX)[:, None], LANES, 1).astype(np.float32)

    rows = np.zeros((3, ZP))
    rows[0, :CZ] = c1
    rows[1, :CZ] = c2
    rows[2, :CZ] = kap
    levels = np.repeat(rows.reshape(-1)[:, None], LANES, 1).astype(np.float32)
    consts = dict(
        c1=[float(a) for a in c1], c2=[float(a) for a in c2],
        stay=[float(a) for a in 0.248 * (1.0 - 2.0 * k)], move=[float(a) for a in 0.248 * k],
        s11=float((kap * c1 * c1).sum()), s12=float((kap * c1 * c2).sum()), s22=float((kap * c2 * c2).sum()),
        sc1=float((kap * c1).sum()), sc2=float((kap * c2).sum()))
    return maps, tail, passive, drift, levels, consts


def halves(x):
    high = x.astype(BF16)
    return high, (x - high.astype(F32)).astype(BF16)


def dot(a, b):
    return lax.dot_general(a, b, (((1,), (0,)), ((), ())), preferred_element_type=F32)


def dot_t(a, b):
    return lax.dot_general(a, b, (((1,), (1,)), ((), ())), preferred_element_type=F32)


class Whole:
    @staticmethod
    def rows(ref, j):
        return jnp.stack([ref[pl.ds(CX * j + v, 8, stride=4), :] for v in range(4)], 0)

    @staticmethod
    def east(f):
        return jnp.concatenate([f[1:], pltpu.roll(f[0], 7, 0)[None]], 0)

    @staticmethod
    def west(f):
        return jnp.concatenate([pltpu.roll(f[3], 1, 0)[None], f[:3]], 0)

    @staticmethod
    def fold(f):
        return (f[0] + f[1]) + (f[2] + f[3])

    @staticmethod
    def join(f):
        return f

    @staticmethod
    def store(ref, i, f):
        for v in range(4):
            ref[pl.ds(CX * i + v, 8, stride=4), :] = f[v]


class Half:
    @staticmethod
    def rows(ref, j):
        low = lax.broadcasted_iota(jnp.int32, (1, LANES), 1) < EDGE
        return jnp.stack([
            jnp.where(low, ref[pl.ds(CX * j + v, 8, stride=2), :], ref[pl.ds(CX * j + 16 + v, 8, stride=2), :])
            for v in range(2)], 0)

    @staticmethod
    def east(f):
        near = pltpu.roll(f[0], 7, 0)
        edge = lax.broadcasted_iota(jnp.int32, (8, LANES), 0) == 7
        return jnp.stack([f[1], jnp.where(edge, swap(near), near)], 0)

    @staticmethod
    def west(f):
        near = pltpu.roll(f[1], 1, 0)
        edge = lax.broadcasted_iota(jnp.int32, (8, LANES), 0) == 0
        return jnp.stack([jnp.where(edge, swap(near), near), f[0]], 0)

    @staticmethod
    def fold(f):
        return f[0] + f[1]

    @staticmethod
    def join(f):
        return f + swap(f)

    @staticmethod
    def store(ref, i, f):
        low = lax.broadcasted_iota(jnp.int32, (1, LANES), 1) < EDGE
        for v in range(2):
            other = swap(f[v])
            ref[pl.ds(CX * i + v, 8, stride=2), :] = jnp.where(low, f[v], other)
            ref[pl.ds(CX * i + 16 + v, 8, stride=2), :] = jnp.where(low, other, f[v])


def swap(x):
    return pltpu.roll(x, EDGE, 1)


def prepare(form, sur_ref):
    east, west = form.east, form.west
    r0, r1, s2 = form.rows(sur_ref, 0), form.rows(sur_ref, 1), form.rows(sur_ref, 2)
    sy, sw = (r1 - 0.3 * r0) * (1.0 / 0.62), r0 + 0.8 * r1

    def xsum(f):
        return form.join(jnp.sum(form.fold(f), axis=0, keepdims=True))

    def parts(s):
        e, w = east(s), west(s)
        return 0.6 * s + 0.2 * (e + w), e - w

    ay, dy = parts(sy)
    a2, d2 = parts(s2)
    af, df = -0.25 * a2, -0.25 * d2
    aw, dw = parts(sw)
    ew, ef = s2 * dw, s2 * df
    haw, hdw, hew = east(aw) - west(aw), east(dw) - west(dw), east(ew) - west(ew)
    gram = (xsum(af * haw), xsum(af * hdw + df * haw), xsum(af * hew + ef * haw),
            xsum(df * hdw), xsum(df * hew + ef * hdw), xsum(ef * hew))
    means = (xsum(sw) * (1.0 / CX), xsum(ew) * (1.0 / CX))
    return s2, ay, dy, af, df, aw, dw, ef, haw, hdw, hew, gram, means


def cloud(form, consts, prep, prof_ref, lanes, tail_ref, lev_ref, part_ref, diag_ref):
    s2, ay, dy, af, df, aw, dw, ef, haw, hdw, hew, gram, means = prep
    east, west = form.east, form.west

    def level(start, z):
        return prof_ref[start + z:start + z + 1, lanes][None]

    def horizontal(z):
        turn = level(128, z) + consts["c2"][z] * s2
        y = (level(0, z) + consts["c1"][z] * ay) + turn * dy
        pull = (level(64, z) + consts["c1"][z] * af) + turn * df
        one = jnp.log(1.0 + jnp.exp2(y * (0.62 * math.log2(math.e))))
        y = y - one
        e, w = east(y), west(y)
        return (1.5 * y + w) + pull * (e - w), one

    def vertical(z, h, above, below):
        v = consts["stay"][z] * h + consts["move"][z] * (above + below)
        two = jnp.maximum(jnp.log(1.0 + jnp.exp(jnp.minimum(v, 80.0))), v)
        part_ref[8 * z:8 * z + 8, :] = form.fold(v) - 0.62 * form.fold(two)
        return v, two

    h, rain = horizontal(0)
    below = h
    total_v = total_2 = None
    for z in range(CZ):
        if z + 1 < CZ:
            above, one = horizontal(z + 1)
            rain = rain + one
        else:
            above = h
        v, two = vertical(z, h, above, below)
        total_v = v if z == 0 else total_v + v
        total_2 = two if z == 0 else total_2 + two
        h, below = above, h
    sum_y = total_v - 0.62 * total_2

    pf = prof_ref[64:128, lanes] - 0.5
    q = prof_ref[128:192, lanes]
    s1p, s2p, s1q, sq2, sq, spw, sb = [prof_ref[336 + i:337 + i, lanes] for i in range(7)]
    c1 = lev_ref[0:ZP, :]
    c2 = lev_ref[ZP:2 * ZP, :]
    kap = lev_ref[2 * ZP:3 * ZP, :]
    g11, g12, g13, g22, g23, g33 = gram
    bend = c1 * (c1 * g11 + q * g12 + c2 * g13) + q * (q * g22 + c2 * g23) + (c2 * c2) * g33
    mean_w = c1 * means[0] + c2 * means[1] + (0.4 / CX) * bend
    qk = q * kap
    sqp = jnp.sum(qk * pf, axis=0, keepdims=True)
    sqq = jnp.sum(qk * q, axis=0, keepdims=True)
    s11, s12, s22 = consts["s11"], consts["s12"], consts["s22"]
    w1 = (spw + consts["sc1"] * aw) + (sq * dw + consts["sc2"] * (s2 * dw))
    sum_w = (
        (0.6 * w1 + 0.2 * (east(w1) + west(w1)))
        + 0.4 * (
            haw * ((s1p + s11 * af) + (s1q * df + s12 * ef))
            + hdw * ((sqp + s1q * af) + (sqq * df + sq2 * ef))
            + hew * ((s2p + s12 * af) + (sq2 * df + s22 * ef))
        )
    )
    form.store(diag_ref, 0, 0.5 * (rain + total_2))
    form.store(diag_ref, 1, (sum_y + 0.3 * sum_w) * (1.0 / (1.24 * CZ)))
    form.store(diag_ref, 2, (sum_w - 0.8 * sum_y) * (1.0 / (1.24 * CZ)) - sb * (1.0 / CZ))

    mean_y = part_ref[pl.ds(0, CZ, stride=8), :]
    for s in range(1, 8):
        mean_y = mean_y + part_ref[pl.ds(s, CZ, stride=8), :]
    mean_y = form.join(mean_y) * (1.0 / CX)
    hi, lo = halves(jnp.concatenate([mean_w, mean_y, jnp.zeros((ZP - CZ, LANES), F32)], 0))
    return prof_ref[192:336, lanes] + dot(tail_ref[...], jnp.concatenate([hi, hi, lo], 0))


PARTS = ((slice(0, 112), slice(8, 64)), (slice(112, 224), slice(64, 120)), (slice(224, 288), slice(120, 152)))
SENT = ((0, 64), (64, 56), (120, 32))


def kernel(consts, n_elem, state_ref, surface_ref, mass_hbm, active_hbm, maps_hbm, tail_hbm, passive_hbm,
           drift_hbm, lev_hbm, out_ref, diag_out_ref,
           xs, hi_ref, lo_ref, su, ones_ref, send, recv, sur, prof, edge_prof, part, diag, both_hi, both_lo, own_ref,
           mass_ref, active_ref, maps_ref, tail_ref, passive_ref, drift_ref, lev_ref,
           in_sem, send_sem, recv_sem):
    e, g = lax.axis_index("elem"), lax.axis_index("grp")
    after = lax.rem(e + 1, n_elem)
    before = lax.rem(e + n_elem - 1, n_elem)
    barrier = pltpu.get_barrier_semaphore()
    for other in (before, after):
        pl.semaphore_signal(barrier, inc=1, device_id=(other, g), device_id_type=MESH)

    tiles = [slice(LANES * b, LANES * (b + 1)) for b in range(4)]
    ends = (tiles[3], tiles[0])
    loads = [
        pltpu.make_async_copy(state_ref.at[rows, lanes], xs.at[rows, lanes], in_sem.at[2 * c + i])
        for c, (rows, _) in enumerate(PARTS) for i, lanes in enumerate(ends)
    ] + [
        pltpu.make_async_copy(state_ref.at[:, pl.ds(LANES, 2 * LANES)], xs.at[:, pl.ds(LANES, 2 * LANES)], in_sem.at[6]),
        pltpu.make_async_copy(surface_ref, su, in_sem.at[7]),
    ]
    small = [
        pltpu.make_async_copy(a, b, in_sem.at[8 + i])
        for i, (a, b) in enumerate((
            (mass_hbm, mass_ref), (active_hbm, active_ref), (maps_hbm, maps_ref), (lev_hbm, lev_ref),
            (tail_hbm, tail_ref), (passive_hbm, passive_ref), (drift_hbm, drift_ref)))
    ]
    for load in small[:1] + loads[:6] + small[1:2] + loads[6:] + small[2:]:
        load.start()

    low = lax.broadcasted_iota(jnp.int32, (1, LANES), 1) < EDGE
    sides = (~low, low)

    def twice(x, i):
        return jnp.where(sides[i], x, swap(x))

    sent = [
        pltpu.make_async_remote_copy(
            src_ref=send.at[i, pl.ds(*rows)], dst_ref=recv.at[i, pl.ds(*rows)],
            send_sem=send_sem.at[2 * c + i], recv_sem=recv_sem.at[2 * c + i],
            device_id=(other, g), device_id_type=MESH)
        for c, rows in enumerate(SENT) for i, other in enumerate((after, before))
    ]

    def enter():
        pl.semaphore_wait(barrier, 2)

    pl.when(e != 0)(enter)
    small[0].wait()
    for c, (rows, to) in enumerate(PARTS):
        for i, lanes in enumerate(ends):
            if c == 0:
                send[i, 0:8, :] = jnp.broadcast_to(twice(mass_ref[:, lanes], i), (8, LANES))
            loads[2 * c + i].wait()
            x = xs[rows, lanes]
            a, b = x[:x.shape[0] // 2], x[x.shape[0] // 2:]
            send[i, to, :] = jnp.where(low, swap(a), b) if i == 0 else jnp.where(low, a, swap(b))
            pl.when(e != 0)(sent[2 * c + i].start)

    small[1].wait()
    act = [active_ref[:, lanes].astype(F32) for lanes in tiles]
    inner = [jnp.where(low, 0.0, act[0]), act[1], act[2], jnp.where(low, act[3], 0.0)]
    marks = jnp.concatenate(inner + [jnp.zeros((4, LANES), F32)], 0)
    r = lax.broadcasted_iota(jnp.int32, (LANES, LANES), 0)
    c = lax.broadcasted_iota(jnp.int32, (LANES, LANES), 1)
    tri = jnp.where(r <= c, 1.0, 0.0).astype(BF16)
    counts = dot(marks.astype(BF16), jnp.concatenate([tri, jnp.ones((LANES, LANES), BF16)], 1))
    where = lax.broadcasted_iota(jnp.int32, (2 * BLOCK, LANES), 0).astype(F32)
    offset = jnp.full((1, LANES), -1.0, F32)
    for b, lanes in enumerate(tiles):
        place = jnp.where(inner[b] > 0.5, counts[b:b + 1, :LANES] + offset, -1.0)
        ones_ref[:, lanes] = jnp.where(where == place, 1.0, 0.0).astype(BF16)
        offset = offset + counts[b:b + 1, LANES:]

    loads[6].wait()
    loads[7].wait()
    hi, lo = halves(xs[...])
    hi_ref[0:288, :] = hi
    lo_ref[0:288, :] = lo
    hi, lo = halves(su[...])
    hi_ref[288:384, :] = hi
    lo_ref[288:384, :] = lo
    for load in small[2:]:
        load.wait()

    def gather(ref, rows):
        return dot_t(ref[rows, :], ones_ref[...])

    def maps(hi, lo):
        x = dot(maps_ref[...], jnp.concatenate([hi, hi, lo], 0))
        return jnp.concatenate([x[:64], x[64:128] + 0.5, x[128:]], 0)

    main = slice(0, STATE_ROWS)
    prof[...] = maps(gather(hi_ref, main).astype(BF16), gather(lo_ref, main).astype(BF16))
    found = gather(hi_ref, slice(288, 384)) + gather(lo_ref, slice(288, 384))
    for i in range(2):
        lanes = tiles[i]
        sur[...] = found[:, lanes]
        tend = cloud(Whole, consts, prepare(Whole, sur), prof, lanes, tail_ref, lev_ref, part, diag)
        hi, lo = halves(jnp.concatenate([tend, diag[...]], 0))
        both_hi[:, lanes] = hi
        both_lo[:, lanes] = lo

    @pl.when(e == 0)
    def _():
        enter()
        for copy in sent:
            copy.start()

    def passive(lanes, hi, lo):
        slow = dot(passive_ref[...], jnp.concatenate([hi, hi, lo], 0))
        mean2 = jnp.sum(su[2 * CX:3 * CX, lanes], axis=0, keepdims=True)
        return jnp.concatenate([slow[:LEV] + drift_ref[...] * mean2, slow[LEV:]], 0)

    for b, lanes in enumerate(tiles):
        out_ref[HALF:, lanes] = xs[HALF:, lanes] + jnp.where(
            act[b] > 0.5, passive(lanes, hi_ref[HALF:288, lanes], lo_ref[HALF:288, lanes]), 0.0)
    back = dot(both_hi[...], ones_ref[...]) + dot(both_lo[...], ones_ref[...])
    out_ref[0:HALF, :] = xs[0:HALF, :] + back[0:HALF]
    diag_out_ref[...] = back[HALF:]

    for i, lanes in enumerate(ends):
        got = 1 - i
        sur[...] = twice(su[:, lanes], i)
        prep = prepare(Half, sur)
        own_ref[...] = twice(xs[:, lanes], i)
        own_mass = twice(mass_ref[:, lanes], i)
        on = jnp.where(sides[i], act[3 if i == 0 else 0], 0.0) > 0.5

        def shared(c, share, rest):
            rows, to = PARTS[c]
            x = recv[got, to, :]
            y = swap(x)
            x = jnp.concatenate([jnp.where(low, x, y), jnp.where(low, y, x)], 0)
            return own_ref[rows, :] * share + x * rest

        sent[got].wait_recv()
        sent[2 + got].wait_recv()
        other_mass = recv[got, 0:1, :]
        scale = 1.0 / (own_mass + other_mass)
        share, rest = own_mass * scale, other_mass * scale
        first = jnp.concatenate([shared(0, share, rest), shared(1, share, rest)], 0)
        hi, lo = halves(first)
        edge_prof[...] = maps(hi, lo)
        tend = cloud(Half, consts, prep, edge_prof, tiles[0], tail_ref, lev_ref, part, diag)
        sent[4 + got].wait_recv()
        last = shared(2, share, rest)
        last_hi, last_lo = halves(last)
        slow = passive(lanes, jnp.concatenate([hi[HALF:], last_hi], 0), jnp.concatenate([lo[HALF:], last_lo], 0))
        new = jnp.concatenate([first, last], 0) + jnp.where(on, jnp.concatenate([tend, slow], 0), 0.0)
        out_ref[:, lanes] = jnp.where(sides[i], new, out_ref[:, lanes])
        diag_out_ref[:, lanes] = jnp.where(sides[i], jnp.where(on, diag[...], 0.0), diag_out_ref[:, lanes])

    for copy in sent:
        copy.wait_send()


def write(state_ref, diag_ref, state_out, diag_out, sem):
    copies = [pltpu.make_async_copy(state_ref, state_out, sem.at[0]),
              pltpu.make_async_copy(diag_ref, diag_out, sem.at[1])]
    for copy in copies:
        copy.start()
    for copy in copies:
        copy.wait()


def body(n_elem, state, surface, mass, plan, active):
    cols = state.shape[2]
    maps, tail, passive, drift, levels, consts = tables()
    hbm = pl.BlockSpec(memory_space=pltpu.HBM)
    vmem = pl.BlockSpec(memory_space=pltpu.VMEM)
    state, surface, mass, active, maps, tail, passive, drift, levels = [
        pltpu.with_memory_space_constraint(x, pltpu.HBM) for x in (
            state.reshape(4 * LEV, cols), surface.reshape(3 * CX, cols), mass.reshape(1, cols),
            active.reshape(1, cols), *map(jnp.asarray, (maps, tail, passive, drift, levels)))]
    new_state, diag = pl.pallas_call(
        functools.partial(kernel, consts, n_elem),
        out_shape=(pltpu.VMEM((4 * LEV, cols), F32), pltpu.VMEM((3 * CX, cols), F32)),
        in_specs=[hbm] * 9,
        out_specs=(vmem, vmem),
        scratch_shapes=[
            pltpu.VMEM((4 * LEV, cols), F32),
            pltpu.VMEM((384, cols), BF16),
            pltpu.VMEM((384, cols), BF16),
            pltpu.VMEM((3 * CX, cols), F32),
            pltpu.VMEM((2 * BLOCK, cols), BF16),
            pltpu.VMEM((2, HALF + 8, LANES), F32),
            pltpu.VMEM((2, HALF + 8, LANES), F32),
            pltpu.VMEM((3 * CX, BLOCK), F32),
            pltpu.VMEM((352, 2 * BLOCK), F32),
            pltpu.VMEM((352, BLOCK), F32),
            pltpu.VMEM((ZP * 8, BLOCK), F32),
            pltpu.VMEM((3 * CX, BLOCK), F32),
            pltpu.VMEM((HALF + 3 * CX, 2 * BLOCK), BF16),
            pltpu.VMEM((HALF + 3 * CX, 2 * BLOCK), BF16),
            pltpu.VMEM((4 * LEV, LANES), F32),
            pltpu.VMEM((1, cols), F32),
            pltpu.VMEM((1, cols), jnp.int32),
            pltpu.VMEM(maps.shape, BF16),
            pltpu.VMEM(tail.shape, BF16),
            pltpu.VMEM(passive.shape, BF16),
            pltpu.VMEM(drift.shape, F32),
            pltpu.VMEM(levels.shape, F32),
            pltpu.SemaphoreType.DMA((15,)),
            pltpu.SemaphoreType.DMA((6,)),
            pltpu.SemaphoreType.DMA((6,)),
        ],
        compiler_params=pltpu.CompilerParams(
            collective_id=0, has_side_effects=True, vmem_limit_bytes=32 * 1024 * 1024),
    )(
        state, surface, mass, active, maps, tail, passive, drift, levels,
    )
    new_state, diag = pl.pallas_call(
        write,
        out_shape=(jax.ShapeDtypeStruct(new_state.shape, F32), jax.ShapeDtypeStruct(diag.shape, F32)),
        in_specs=[vmem, vmem],
        out_specs=(hbm, hbm),
        scratch_shapes=[pltpu.SemaphoreType.DMA((2,))],
    )(pltpu.with_memory_space_constraint(new_state, pltpu.VMEM), pltpu.with_memory_space_constraint(diag, pltpu.VMEM))
    return new_state.reshape(4, LEV, cols), diag.reshape(3, CX, cols)


def solution(mesh):
    both = ("elem", "grp")
    return jax.shard_map(
        functools.partial(body, mesh.shape["elem"]),
        mesh=mesh,
        in_specs=(P(None, None, both), P(None, None, both), P(both), P(None, both), P(both)),
        out_specs=(P(None, None, both), P(None, None, both)),
        check_vma=False,
    )
```

time: 13.8 us -> 13 us (0.942)
  the two profiles are of different devices: /device:TPU:0 before, /device:TPU:1 now
where the time goes in v2:
time: 13 us; the launch traced here: 12.9 us
  Pallas kernels  12.2 us (94%)
  between operations  0.64 us (5%)
    pallas_call x1, Pallas kernels, body(): pl.pallas_call(functools.partial(kernel, consts, n_elem), out_shape=(pltp...  11.3 us
    pallas_call x1, Pallas kernels, body(): pl.pallas_call(write, out_shape=(jax.ShapeDtypeStruct(new_state.shape, F3...  0.89 us

profile of v2, /device:TPU:1, one launch (start us, length us, event | category | flops | bytes accessed | tf_op | source)
XLA Modules:
  0.0 12.9 jit_solution(14856864704541013646)
XLA Ops:
  0.6 11.3 %shard_map.104 = (f32[288,512]{1,0:T(8,128)S(1)}, f32[96,512]{1,0:T(8,128)S(1)}) custom-call(f32[288,512]{1,0:T(8,128)} %bitcast.6, f32[96,512]{1,0:T(8,128)} %bitcast.7, f32[1,512]{1,0:T(1,128)} %bitcast.8, s32[1,512]{1,0:T(1,128)} %bitcast.9, bf16[352,672]{1,0:T(8,128)(2,1)} %constant.10.clone.maps_hbm, bf16[144,384]{1,0:T(8,128)(2,1)} %constant.11.clone.tail_hbm, ...), custom_call_target="tpu_custom_call" | custom-call | tf_op jit(solution)/shard_map/pallas_call | solution.py:457
  12.0 0.9 %shard_map.105 = (f32[288,512]{1,0:T(8,128)}, f32[96,512]{1,0:T(8,128)}) custom-call(f32[288,512]{1,0:T(8,128)S(1)} %get-tuple-element.6.state_ref, f32[96,512]{1,0:T(8,128)S(1)} %get-tuple-element.7.diag_ref), custom_call_target="tpu_custom_call" | custom-call | tf_op jit(solution)/shard_map/pallas_call | solution.py:494

commit v3 on v2

--- a/solution.py
+++ b/solution.py
@@ -48,28 +48,29 @@
     kb = mix @ up
     qb = -0.1 * (mix @ (fall[:, None] * up))
 
-    m = np.zeros((344, STATE_ROWS))
-    p0, p1, p2 = slice(0, 72), slice(72, 144), slice(144, 216)
-    m[0:CZ, p1] = kb / 0.62
-    m[0:CZ, p0] = -0.3 * kb / 0.62
+    py, p2, p0 = slice(0, 72), slice(72, 144), slice(144, 216)
+    m = np.zeros((208, HALF))
+    m[0:CZ, py] = kb / 0.62
     m[64:64 + CZ, p2] = -0.25 * kb
     m[128:128 + CZ, p2] = qb
-    dkk = down @ mix @ kb
-    m[192:264, p0] = dkk / 1.24 - down @ up
-    m[192:264, p1] = 0.8 * dkk / 1.24
-    m[264:336, p0] = 0.3 * dkk / 1.24
-    m[264:336, p1] = 0.3 * 0.8 * dkk / 1.24 - down @ up
-    m[336, p2] = (kap * c1) @ (-0.25 * kb)
-    m[337, p2] = (kap * c2) @ (-0.25 * kb)
-    m[338, p2] = (kap * c1) @ qb
-    m[339, p2] = (kap * c2) @ qb
-    m[340, p2] = kap @ qb
-    m[341, p0] = kap @ kb
-    m[341, p1] = 0.8 * (kap @ kb)
-    m[342, p0] = up.sum(0)
+    m[192, p2] = (kap * c1) @ (-0.25 * kb)
+    m[193, p2] = (kap * c2) @ (-0.25 * kb)
+    m[194, p2] = (kap * c1) @ qb
+    m[195, p2] = (kap * c2) @ qb
+    m[196, p2] = kap @ qb
     hi, lo = split_np(m)
     maps = np.concatenate([hi, lo, hi], 1)
-    maps = np.concatenate([maps, np.zeros((8, maps.shape[1]), maps.dtype)], 0)
+    dkk = down @ mix @ kb
+    m = np.zeros((160, STATE_ROWS))
+    m[0:72, p0] = dkk - down @ up
+    m[0:72, py] = 0.8 * dkk / 1.24
+    m[72:144, p0] = 0.3 * (dkk - down @ up)
+    m[72:144, py] = 0.24 * dkk / 1.24 - down @ up
+    m[144, p0] = 1.24 * (kap @ kb)
+    m[144, py] = 0.8 * (kap @ kb)
+    m[145, p0] = up.sum(0)
+    hi, lo = split_np(m)
+    more = np.concatenate([hi, lo, hi], 1)
 
     t = np.zeros((HALF, 2 * ZP))
     t[0:72, 0:CZ] = down @ mix / 1.24
@@ -96,7 +97,7 @@
         stay=[float(a) for a in 0.248 * (1.0 - 2.0 * k)], move=[float(a) for a in 0.248 * k],
         s11=float((kap * c1 * c1).sum()), s12=float((kap * c1 * c2).sum()), s22=float((kap * c2 * c2).sum()),
         sc1=float((kap * c1).sum()), sc2=float((kap * c2).sum()))
-    return maps, tail, passive, drift, levels, consts
+    return maps, more, tail, passive, drift, levels, consts
 
 
 def halves(x):
@@ -204,7 +205,7 @@
     return s2, ay, dy, af, df, aw, dw, ef, haw, hdw, hew, gram, means
 
 
-def cloud(form, consts, prep, prof_ref, lanes, tail_ref, lev_ref, part_ref, diag_ref):
+def cloud(form, consts, prep, prof_ref, lanes, tail_ref, lev_ref, part_ref, diag_ref, at={}):
     s2, ay, dy, af, df, aw, dw, ef, haw, hdw, hew, gram, means = prep
     east, west = form.east, form.west
 
@@ -230,6 +231,8 @@
     below = h
     total_v = total_2 = None
     for z in range(CZ):
+        if z in at:
+            at[z]()
         if z + 1 < CZ:
             above, one = horizontal(z + 1)
             rain = rain + one
@@ -243,7 +246,8 @@
 
     pf = prof_ref[64:128, lanes] - 0.5
     q = prof_ref[128:192, lanes]
-    s1p, s2p, s1q, sq2, sq, spw, sb = [prof_ref[336 + i:337 + i, lanes] for i in range(7)]
+    s1p, s2p, s1q, sq2, sq = [prof_ref[192 + i:193 + i, lanes] for i in range(5)]
+    spw, sb = [prof_ref[352 + i:353 + i, lanes] for i in range(2)]
     c1 = lev_ref[0:ZP, :]
     c2 = lev_ref[ZP:2 * ZP, :]
     kap = lev_ref[2 * ZP:3 * ZP, :]
@@ -272,17 +276,16 @@
         mean_y = mean_y + part_ref[pl.ds(s, CZ, stride=8), :]
     mean_y = form.join(mean_y) * (1.0 / CX)
     hi, lo = halves(jnp.concatenate([mean_w, mean_y, jnp.zeros((ZP - CZ, LANES), F32)], 0))
-    return prof_ref[192:336, lanes] + dot(tail_ref[...], jnp.concatenate([hi, hi, lo], 0))
-
-
-PARTS = ((slice(0, 112), slice(8, 64)), (slice(112, 224), slice(64, 120)), (slice(224, 288), slice(120, 152)))
-SENT = ((0, 64), (64, 56), (120, 32))
-
-
-def kernel(consts, n_elem, state_ref, surface_ref, mass_hbm, active_hbm, maps_hbm, tail_hbm, passive_hbm,
+    return prof_ref[208:352, lanes] + dot(tail_ref[...], jnp.concatenate([hi, hi, lo], 0))
+
+
+SENT = ((0, 80), (80, 72))
+
+
+def kernel(consts, n_elem, state_ref, surface_ref, mass_hbm, active_hbm, maps_hbm, more_hbm, tail_hbm, passive_hbm,
            drift_hbm, lev_hbm, out_ref, diag_out_ref,
            xs, hi_ref, lo_ref, su, ones_ref, send, recv, sur, prof, edge_prof, part, diag, both_hi, both_lo, own_ref,
-           mass_ref, active_ref, maps_ref, tail_ref, passive_ref, drift_ref, lev_ref,
+           mass_ref, active_ref, maps_ref, more_ref, tail_ref, passive_ref, drift_ref, lev_ref,
            in_sem, send_sem, recv_sem):
     e, g = lax.axis_index("elem"), lax.axis_index("grp")
     after = lax.rem(e + 1, n_elem)
@@ -294,49 +297,57 @@
     tiles = [slice(LANES * b, LANES * (b + 1)) for b in range(4)]
     ends = (tiles[3], tiles[0])
     loads = [
-        pltpu.make_async_copy(state_ref.at[rows, lanes], xs.at[rows, lanes], in_sem.at[2 * c + i])
-        for c, (rows, _) in enumerate(PARTS) for i, lanes in enumerate(ends)
+        pltpu.make_async_copy(state_ref.at[rows, lanes], xs.at[rows, lanes], in_sem.at[k])
+        for k, (rows, lanes) in enumerate(
+            (rows, lanes) for rows in (slice(0, 3 * LEV), slice(3 * LEV, 4 * LEV)) for lanes in ends)
     ] + [
-        pltpu.make_async_copy(state_ref.at[:, pl.ds(LANES, 2 * LANES)], xs.at[:, pl.ds(LANES, 2 * LANES)], in_sem.at[6]),
-        pltpu.make_async_copy(surface_ref, su, in_sem.at[7]),
+        pltpu.make_async_copy(state_ref.at[:, pl.ds(LANES, 2 * LANES)], xs.at[:, pl.ds(LANES, 2 * LANES)], in_sem.at[4]),
+        pltpu.make_async_copy(surface_ref, su, in_sem.at[5]),
     ]
     small = [
-        pltpu.make_async_copy(a, b, in_sem.at[8 + i])
+        pltpu.make_async_copy(a, b, in_sem.at[6 + i])
         for i, (a, b) in enumerate((
             (mass_hbm, mass_ref), (active_hbm, active_ref), (maps_hbm, maps_ref), (lev_hbm, lev_ref),
-            (tail_hbm, tail_ref), (passive_hbm, passive_ref), (drift_hbm, drift_ref)))
+            (more_hbm, more_ref), (tail_hbm, tail_ref), (passive_hbm, passive_ref), (drift_hbm, drift_ref)))
     ]
-    for load in small[:1] + loads[:6] + small[1:2] + loads[6:] + small[2:]:
+    for load in small[:1] + loads[:4] + small[1:2] + loads[4:] + small[2:]:
         load.start()
 
     low = lax.broadcasted_iota(jnp.int32, (1, LANES), 1) < EDGE
-    sides = (~low, low)
-
-    def twice(x, i):
-        return jnp.where(sides[i], x, swap(x))
-
-    sent = [
-        pltpu.make_async_remote_copy(
-            src_ref=send.at[i, pl.ds(*rows)], dst_ref=recv.at[i, pl.ds(*rows)],
+
+    def end_copy(c, i):
+        rows = pl.ds(*SENT[c])
+        return pltpu.make_async_remote_copy(
+            src_ref=send.at[i, rows], dst_ref=recv.at[i, rows],
             send_sem=send_sem.at[2 * c + i], recv_sem=recv_sem.at[2 * c + i],
-            device_id=(other, g), device_id_type=MESH)
-        for c, rows in enumerate(SENT) for i, other in enumerate((after, before))
-    ]
+            device_id=((after, before)[i] if isinstance(i, int) else after, g), device_id_type=MESH)
+
+    sent = [end_copy(c, i) for i in range(2) for c in range(2)]
 
     def enter():
         pl.semaphore_wait(barrier, 2)
 
-    pl.when(e != 0)(enter)
+    def exchange():
+        enter()
+        for copy in sent:
+            copy.start()
+
+    first_e, last_e = e == 0, e == n_elem - 1
+    pl.when(last_e)(enter)
     small[0].wait()
-    for c, (rows, to) in enumerate(PARTS):
-        for i, lanes in enumerate(ends):
-            if c == 0:
-                send[i, 0:8, :] = jnp.broadcast_to(twice(mass_ref[:, lanes], i), (8, LANES))
-            loads[2 * c + i].wait()
-            x = xs[rows, lanes]
-            a, b = x[:x.shape[0] // 2], x[x.shape[0] // 2:]
-            send[i, to, :] = jnp.where(low, swap(a), b) if i == 0 else jnp.where(low, a, swap(b))
-            pl.when(e != 0)(sent[2 * c + i].start)
+    for i, lanes in enumerate(ends):
+        mass = mass_ref[:, lanes]
+        mass = jnp.where(low, swap(mass), mass) if i == 0 else jnp.where(low, mass, swap(mass))
+        send[i, 0:8, :] = jnp.broadcast_to(mass, (8, LANES))
+        loads[i].wait()
+        p0 = xs[0:LEV, lanes]
+        py, p2 = xs[LEV:2 * LEV, lanes] - 0.3 * p0, xs[2 * LEV:3 * LEV, lanes]
+        send[i, 8:80, :] = jnp.where(low, swap(py), p2) if i == 0 else jnp.where(low, py, swap(p2))
+        pl.when(last_e)(sent[2 * i].start)
+        loads[2 + i].wait()
+        p0, p3 = xs[0:LEV, lanes], xs[3 * LEV:, lanes]
+        send[i, 80:152, :] = jnp.where(low, swap(p0), p3) if i == 0 else jnp.where(low, p0, swap(p3))
+        pl.when(last_e)(sent[2 * i + 1].start)
 
     small[1].wait()
     act = [active_ref[:, lanes].astype(F32) for lanes in tiles]
@@ -353,9 +364,14 @@
         ones_ref[:, lanes] = jnp.where(where == place, 1.0, 0.0).astype(BF16)
         offset = offset + counts[b:b + 1, LANES:]
 
-    loads[6].wait()
-    loads[7].wait()
-    hi, lo = halves(xs[...])
+    loads[4].wait()
+    loads[5].wait()
+
+    def ordered(x):
+        return jnp.concatenate(
+            [x[LEV:2 * LEV] - 0.3 * x[0:LEV], x[2 * LEV:3 * LEV], x[0:LEV], x[3 * LEV:4 * LEV]], 0)
+
+    hi, lo = halves(ordered(xs[...]))
     hi_ref[0:288, :] = hi
     lo_ref[0:288, :] = lo
     hi, lo = halves(su[...])
@@ -363,74 +379,138 @@
     lo_ref[288:384, :] = lo
     for load in small[2:]:
         load.wait()
+    pl.when(jnp.logical_and(e > 1, e < n_elem - 1))(exchange)
 
     def gather(ref, rows):
         return dot_t(ref[rows, :], ones_ref[...])
 
-    def maps(hi, lo):
+    def first_maps(ref, hi, lo):
         x = dot(maps_ref[...], jnp.concatenate([hi, hi, lo], 0))
-        return jnp.concatenate([x[:64], x[64:128] + 0.5, x[128:]], 0)
-
+        ref[0:64, :] = x[:64]
+        ref[64:128, :] = x[64:128] + 0.5
+        ref[128:208, :] = x[128:]
+
+    def more_maps(ref, hi, lo):
+        ref[208:368, :] = dot(more_ref[...], jnp.concatenate([hi, hi, lo], 0))
+
+    def to_next():
+        for c in range(2):
+            end_copy(c, 1).wait_recv()
+        sent[0].start()
+        sent[1].start()
+
+    def to_previous():
+        enter()
+        sent[2].start()
+        sent[3].start()
+
+    meanwhile = ({24: lambda: pl.when(e == 1)(exchange)}, {8: lambda: pl.when(first_e)(to_next)})
     main = slice(0, STATE_ROWS)
-    prof[...] = maps(gather(hi_ref, main).astype(BF16), gather(lo_ref, main).astype(BF16))
+    hi, lo = gather(hi_ref, main).astype(BF16), gather(lo_ref, main).astype(BF16)
+    first_maps(prof, hi[:HALF], lo[:HALF])
+    more_maps(prof, hi, lo)
     found = gather(hi_ref, slice(288, 384)) + gather(lo_ref, slice(288, 384))
     for i in range(2):
         lanes = tiles[i]
         sur[...] = found[:, lanes]
-        tend = cloud(Whole, consts, prepare(Whole, sur), prof, lanes, tail_ref, lev_ref, part, diag)
+        tend = cloud(Whole, consts, prepare(Whole, sur), prof, lanes, tail_ref, lev_ref, part, diag, meanwhile[i])
         hi, lo = halves(jnp.concatenate([tend, diag[...]], 0))
         both_hi[:, lanes] = hi
         both_lo[:, lanes] = lo
 
-    @pl.when(e == 0)
-    def _():
-        enter()
-        for copy in sent:
-            copy.start()
-
-    def passive(lanes, hi, lo):
+    pl.when(first_e)(to_previous)
+
+    def passive(x, s2):
+        hi, lo = halves(x)
         slow = dot(passive_ref[...], jnp.concatenate([hi, hi, lo], 0))
-        mean2 = jnp.sum(su[2 * CX:3 * CX, lanes], axis=0, keepdims=True)
+        mean2 = jnp.sum(s2, axis=0, keepdims=True)
         return jnp.concatenate([slow[:LEV] + drift_ref[...] * mean2, slow[LEV:]], 0)
 
     for b, lanes in enumerate(tiles):
-        out_ref[HALF:, lanes] = xs[HALF:, lanes] + jnp.where(
-            act[b] > 0.5, passive(lanes, hi_ref[HALF:288, lanes], lo_ref[HALF:288, lanes]), 0.0)
+        x = xs[HALF:, lanes]
+        out_ref[HALF:, lanes] = x + jnp.where(act[b] > 0.5, passive(x, su[2 * CX:, lanes]), 0.0)
     back = dot(both_hi[...], ones_ref[...]) + dot(both_lo[...], ones_ref[...])
     out_ref[0:HALF, :] = xs[0:HALF, :] + back[0:HALF]
     diag_out_ref[...] = back[HALF:]
 
-    for i, lanes in enumerate(ends):
-        got = 1 - i
-        sur[...] = twice(su[:, lanes], i)
-        prep = prepare(Half, sur)
-        own_ref[...] = twice(xs[:, lanes], i)
-        own_mass = twice(mass_ref[:, lanes], i)
-        on = jnp.where(sides[i], act[3 if i == 0 else 0], 0.0) > 0.5
-
-        def shared(c, share, rest):
-            rows, to = PARTS[c]
-            x = recv[got, to, :]
+    def edge(form, own_mass, on, wait, other_mass, arrived):
+        prep = prepare(form, sur)
+        wait(0)
+        masses = other_mass()
+        scale = 1.0 / (own_mass + masses)
+        share, rest = own_mass * scale, masses * scale
+        start = own_ref[0:HALF, :] * share + arrived(8) * rest
+        hi, lo = halves(start)
+        first_maps(edge_prof, hi, lo)
+        keep = []
+
+        def late():
+            wait(1)
+            final = own_ref[HALF:, :] * share + arrived(80) * rest
+            keep.append(final)
+            more_hi, more_lo = halves(final[:80])
+            more_maps(edge_prof, jnp.concatenate([hi, more_hi], 0), jnp.concatenate([lo, more_lo], 0))
+
+        tend = cloud(form, consts, prep, edge_prof, tiles[0], tail_ref, lev_ref, part, diag, {24: late})
+        py, p2, p0, p3 = start[:LEV], start[LEV:], keep[0][:LEV], keep[0][LEV:]
+        slow = passive(jnp.concatenate([p2, p3], 0), sur[2 * CX:, :])
+        shared = jnp.concatenate([p0, py + 0.3 * p0, p2, p3], 0)
+        return shared + jnp.where(on, jnp.concatenate([tend, slow], 0), 0.0), jnp.where(on, diag[...], 0.0)
+
+    def one_end(k, _):
+        i, got = k, 1 - k
+        lanes = pl.ds(pl.multiple_of((1 - i) * (3 * LANES), LANES), LANES)
+        side = low == (i == 1)
+
+        def double(x):
+            return jnp.where(side, x, swap(x))
+
+        def arrived(row):
+            x = recv[got, row:row + LEV, :]
             y = swap(x)
-            x = jnp.concatenate([jnp.where(low, x, y), jnp.where(low, y, x)], 0)
-            return own_ref[rows, :] * share + x * rest
-
-        sent[got].wait_recv()
-        sent[2 + got].wait_recv()
-        other_mass = recv[got, 0:1, :]
-        scale = 1.0 / (own_mass + other_mass)
-        share, rest = own_mass * scale, other_mass * scale
-        first = jnp.concatenate([shared(0, share, rest), shared(1, share, rest)], 0)
-        hi, lo = halves(first)
-        edge_prof[...] = maps(hi, lo)
-        tend = cloud(Half, consts, prep, edge_prof, tiles[0], tail_ref, lev_ref, part, diag)
-        sent[4 + got].wait_recv()
-        last = shared(2, share, rest)
-        last_hi, last_lo = halves(last)
-        slow = passive(lanes, jnp.concatenate([hi[HALF:], last_hi], 0), jnp.concatenate([lo[HALF:], last_lo], 0))
-        new = jnp.concatenate([first, last], 0) + jnp.where(on, jnp.concatenate([tend, slow], 0), 0.0)
-        out_ref[:, lanes] = jnp.where(sides[i], new, out_ref[:, lanes])
-        diag_out_ref[:, lanes] = jnp.where(sides[i], jnp.where(on, diag[...], 0.0), diag_out_ref[:, lanes])
+            return jnp.concatenate([jnp.where(low, x, y), jnp.where(low, y, x)], 0)
+
+        sur[...] = double(su[:, lanes])
+        own_ref[...] = ordered(double(xs[:, lanes]))
+        new, seen = edge(
+            Half, double(mass_ref[:, lanes]), jnp.where(side, active_ref[:, lanes], 0) == 1,
+            lambda c: pl.when(jnp.logical_not(jnp.logical_and(first_e, got == 1)))(end_copy(c, got).wait_recv),
+            lambda: recv[got, 0:1, :], arrived)
+        out_ref[:, lanes] = jnp.where(side, new, out_ref[:, lanes])
+        diag_out_ref[:, lanes] = jnp.where(side, seen, diag_out_ref[:, lanes])
+        return 0
+
+    def both_ends():
+        t0, t3 = tiles[0], tiles[3]
+
+        def merge(ref):
+            return jnp.where(low, ref[:, t0], ref[:, t3])
+
+        def wait(c):
+            for got in range(2):
+                end_copy(c, got).wait_recv()
+
+        def arrived(row):
+            x, y = recv[0, row:row + LEV, :], recv[1, row:row + LEV, :]
+            return jnp.concatenate([jnp.where(low, x, swap(y)), jnp.where(low, swap(x), y)], 0)
+
+        sur[...] = merge(su)
+        own_ref[...] = ordered(merge(xs))
+        new, seen = edge(
+            Whole, merge(mass_ref), merge(active_ref) == 1, wait,
+            lambda: jnp.where(low, recv[0, 0:1, :], recv[1, 0:1, :]), arrived)
+        out_ref[:, t0] = jnp.where(low, new, out_ref[:, t0])
+        out_ref[:, t3] = jnp.where(low, out_ref[:, t3], new)
+        diag_out_ref[:, t0] = jnp.where(low, seen, diag_out_ref[:, t0])
+        diag_out_ref[:, t3] = jnp.where(low, diag_out_ref[:, t3], seen)
+
+    alone = e <= 1
+
+    @pl.when(alone)
+    def _():
+        lax.fori_loop(0, 2, one_end, 0)
+
+    pl.when(jnp.logical_not(alone))(both_ends)
 
     for copy in sent:
         copy.wait_send()
@@ -447,17 +527,17 @@
 
 def body(n_elem, state, surface, mass, plan, active):
     cols = state.shape[2]
-    maps, tail, passive, drift, levels, consts = tables()
+    maps, more, tail, passive, drift, levels, consts = tables()
     hbm = pl.BlockSpec(memory_space=pltpu.HBM)
     vmem = pl.BlockSpec(memory_space=pltpu.VMEM)
-    state, surface, mass, active, maps, tail, passive, drift, levels = [
+    state, surface, mass, active, maps, more, tail, passive, drift, levels = [
         pltpu.with_memory_space_constraint(x, pltpu.HBM) for x in (
             state.reshape(4 * LEV, cols), surface.reshape(3 * CX, cols), mass.reshape(1, cols),
-            active.reshape(1, cols), *map(jnp.asarray, (maps, tail, passive, drift, levels)))]
+            active.reshape(1, cols), *map(jnp.asarray, (maps, more, tail, passive, drift, levels)))]
     new_state, diag = pl.pallas_call(
         functools.partial(kernel, consts, n_elem),
         out_shape=(pltpu.VMEM((4 * LEV, cols), F32), pltpu.VMEM((3 * CX, cols), F32)),
-        in_specs=[hbm] * 9,
+        in_specs=[hbm] * 10,
         out_specs=(vmem, vmem),
         scratch_shapes=[
             pltpu.VMEM((4 * LEV, cols), F32),
@@ -468,8 +548,8 @@
             pltpu.VMEM((2, HALF + 8, LANES), F32),
             pltpu.VMEM((2, HALF + 8, LANES), F32),
             pltpu.VMEM((3 * CX, BLOCK), F32),
-            pltpu.VMEM((352, 2 * BLOCK), F32),
-            pltpu.VMEM((352, BLOCK), F32),
+            pltpu.VMEM((368, 2 * BLOCK), F32),
+            pltpu.VMEM((368, BLOCK), F32),
             pltpu.VMEM((ZP * 8, BLOCK), F32),
             pltpu.VMEM((3 * CX, BLOCK), F32),
             pltpu.VMEM((HALF + 3 * CX, 2 * BLOCK), BF16),
@@ -478,18 +558,19 @@
             pltpu.VMEM((1, cols), F32),
             pltpu.VMEM((1, cols), jnp.int32),
             pltpu.VMEM(maps.shape, BF16),
+            pltpu.VMEM(more.shape, BF16),
             pltpu.VMEM(tail.shape, BF16),
             pltpu.VMEM(passive.shape, BF16),
             pltpu.VMEM(drift.shape, F32),
             pltpu.VMEM(levels.shape, F32),
-            pltpu.SemaphoreType.DMA((15,)),
-            pltpu.SemaphoreType.DMA((6,)),
-            pltpu.SemaphoreType.DMA((6,)),
+            pltpu.SemaphoreType.DMA((14,)),
+            pltpu.SemaphoreType.DMA((4,)),
+            pltpu.SemaphoreType.DMA((4,)),
         ],
         compiler_params=pltpu.CompilerParams(
             collective_id=0, has_side_effects=True, vmem_limit_bytes=32 * 1024 * 1024),
     )(
-        state, surface, mass, active, maps, tail, passive, drift, levels,
+        state, surface, mass, active, maps, more, tail, passive, drift, levels,
     )
     new_state, diag = pl.pallas_call(
         write,

time: 13 us -> 11.9 us (0.915)
  the two profiles are of different devices: /device:TPU:1 before, /device:TPU:0 now
where the time goes in v3:
time: 11.9 us; the launch traced here: 11.8 us
  Pallas kernels  11.2 us (94%)
  between operations  0.64 us (5%)
    pallas_call x1, Pallas kernels, body(): pl.pallas_call(functools.partial(kernel, consts, n_elem), out_shape=(pltp...  10.3 us
    pallas_call x1, Pallas kernels, body(): pl.pallas_call(write, out_shape=(jax.ShapeDtypeStruct(new_state.shape, F3...  0.89 us

profile of v3, /device:TPU:0, one launch (start us, length us, event | category | flops | bytes accessed | tf_op | source)
XLA Modules:
  0.0 11.8 jit_solution(16907966398721674966)
XLA Ops:
  0.6 10.3 %shard_map.113 = (f32[288,512]{1,0:T(8,128)S(1)}, f32[96,512]{1,0:T(8,128)S(1)}) custom-call(f32[288,512]{1,0:T(8,128)} %bitcast.6, f32[96,512]{1,0:T(8,128)} %bitcast.7, f32[1,512]{1,0:T(1,128)} %bitcast.8, s32[1,512]{1,0:T(1,128)} %bitcast.9, bf16[208,432]{1,0:T(8,128)(2,1)} %constant.12.clone.maps_hbm, bf16[160,672]{1,0:T(8,128)(2,1)} %constant.13.clone.more_hbm, ...), custom_call_target="tpu_custom_call" | custom-call | tf_op jit(solution)/shard_map/pallas_call | solution.py:537
  10.9 0.9 %shard_map.114 = (f32[288,512]{1,0:T(8,128)}, f32[96,512]{1,0:T(8,128)}) custom-call(f32[288,512]{1,0:T(8,128)S(1)} %get-tuple-element.6.state_ref, f32[96,512]{1,0:T(8,128)S(1)} %get-tuple-element.7.diag_ref), custom_call_target="tpu_custom_call" | custom-call | tf_op jit(solution)/shard_map/pallas_call | solution.py:575

commit v4 on v3

--- a/solution.py
+++ b/solution.py
@@ -18,7 +18,7 @@
 BLOCK = 128
 ZP = 64
 HALF = 2 * LEV
-STATE_ROWS = 224
+STATE_ROWS = 240
 F32 = jnp.float32
 BF16 = jnp.bfloat16
 MESH = pl.DeviceIdType.MESH
@@ -48,20 +48,20 @@
     kb = mix @ up
     qb = -0.1 * (mix @ (fall[:, None] * up))
 
-    py, p2, p0 = slice(0, 72), slice(72, 144), slice(144, 216)
-    m = np.zeros((208, HALF))
-    m[0:CZ, py] = kb / 0.62
-    m[64:64 + CZ, p2] = -0.25 * kb
-    m[128:128 + CZ, p2] = qb
-    m[192, p2] = (kap * c1) @ (-0.25 * kb)
-    m[193, p2] = (kap * c2) @ (-0.25 * kb)
-    m[194, p2] = (kap * c1) @ qb
-    m[195, p2] = (kap * c2) @ qb
-    m[196, p2] = kap @ qb
+    m = np.zeros((208, 80))
+    m[0:CZ, :LEV] = kb / 0.62
+    m[64:64 + CZ, :LEV] = -0.25 * kb
+    m[128:128 + CZ, :LEV] = qb
+    m[192, :LEV] = (kap * c1) @ (-0.25 * kb)
+    m[193, :LEV] = (kap * c2) @ (-0.25 * kb)
+    m[194, :LEV] = (kap * c1) @ qb
+    m[195, :LEV] = (kap * c2) @ qb
+    m[196, :LEV] = kap @ qb
     hi, lo = split_np(m)
     maps = np.concatenate([hi, lo, hi], 1)
     dkk = down @ mix @ kb
-    m = np.zeros((160, STATE_ROWS))
+    py, p0 = slice(0, 72), slice(80, 152)
+    m = np.zeros((160, 160))
     m[0:72, p0] = dkk - down @ up
     m[0:72, py] = 0.8 * dkk / 1.24
     m[72:144, p0] = 0.3 * (dkk - down @ up)
@@ -72,11 +72,11 @@
     hi, lo = split_np(m)
     more = np.concatenate([hi, lo, hi], 1)
 
-    t = np.zeros((HALF, 2 * ZP))
+    t = np.zeros((2 * HALF, ZP))
     t[0:72, 0:CZ] = down @ mix / 1.24
     t[72:144, 0:CZ] = 0.3 * (down @ mix) / 1.24
-    t[0:72, ZP:ZP + CZ] = -0.8 * down / 1.24
-    t[72:144, ZP:ZP + CZ] = down / 1.24
+    t[144:216, 0:CZ] = -0.8 * down / 1.24
+    t[216:288, 0:CZ] = down / 1.24
     hi, lo = split_np(t)
     tail = np.concatenate([hi, lo, hi], 1)
 
@@ -230,9 +230,39 @@
     h, rain = horizontal(0)
     below = h
     total_v = total_2 = None
+    def passive_sums():
+        pf = prof_ref[64:128, lanes] - 0.5
+        q = prof_ref[128:192, lanes]
+        s1p, s2p, s1q, sq2, sq = [prof_ref[192 + i:193 + i, lanes] for i in range(5)]
+        c1 = lev_ref[0:ZP, :]
+        c2 = lev_ref[ZP:2 * ZP, :]
+        kap = lev_ref[2 * ZP:3 * ZP, :]
+        g11, g12, g13, g22, g23, g33 = gram
+        bend = c1 * (c1 * g11 + q * g12 + c2 * g13) + q * (q * g22 + c2 * g23) + (c2 * c2) * g33
+        mean_w = c1 * means[0] + c2 * means[1] + (0.4 / CX) * bend
+        hi, lo = halves(mean_w)
+        prof_ref[208:352, lanes] += dot(tail_ref[0:HALF, :], jnp.concatenate([hi, hi, lo], 0))
+        qk = q * kap
+        sqp = jnp.sum(qk * pf, axis=0, keepdims=True)
+        sqq = jnp.sum(qk * q, axis=0, keepdims=True)
+        s11, s12, s22 = consts["s11"], consts["s12"], consts["s22"]
+        w1 = (prof_ref[352:353, lanes] + consts["sc1"] * aw) + (sq * dw + consts["sc2"] * (s2 * dw))
+        return (
+            (0.6 * w1 + 0.2 * (east(w1) + west(w1)))
+            + 0.4 * (
+                haw * ((s1p + s11 * af) + (s1q * df + s12 * ef))
+                + hdw * ((sqp + s1q * af) + (sqq * df + sq2 * ef))
+                + hew * ((s2p + s12 * af) + (sq2 * df + s22 * ef))
+            )
+        )
+
     for z in range(CZ):
         if z in at:
             at[z]()
+        if z == 26:
+            sum_w = passive_sums()
+            form.store(diag_ref, 1, 0.3 * sum_w)
+            form.store(diag_ref, 2, sum_w - 1.24 * prof_ref[353:354, lanes])
         if z + 1 < CZ:
             above, one = horizontal(z + 1)
             rain = rain + one
@@ -242,41 +272,31 @@
         total_v = v if z == 0 else total_v + v
         total_2 = two if z == 0 else total_2 + two
         h, below = above, h
-    sum_y = total_v - 0.62 * total_2
-
-    pf = prof_ref[64:128, lanes] - 0.5
-    q = prof_ref[128:192, lanes]
-    s1p, s2p, s1q, sq2, sq = [prof_ref[192 + i:193 + i, lanes] for i in range(5)]
-    spw, sb = [prof_ref[352 + i:353 + i, lanes] for i in range(2)]
-    c1 = lev_ref[0:ZP, :]
-    c2 = lev_ref[ZP:2 * ZP, :]
-    kap = lev_ref[2 * ZP:3 * ZP, :]
-    g11, g12, g13, g22, g23, g33 = gram
-    bend = c1 * (c1 * g11 + q * g12 + c2 * g13) + q * (q * g22 + c2 * g23) + (c2 * c2) * g33
-    mean_w = c1 * means[0] + c2 * means[1] + (0.4 / CX) * bend
-    qk = q * kap
-    sqp = jnp.sum(qk * pf, axis=0, keepdims=True)
-    sqq = jnp.sum(qk * q, axis=0, keepdims=True)
-    s11, s12, s22 = consts["s11"], consts["s12"], consts["s22"]
-    w1 = (spw + consts["sc1"] * aw) + (sq * dw + consts["sc2"] * (s2 * dw))
-    sum_w = (
-        (0.6 * w1 + 0.2 * (east(w1) + west(w1)))
-        + 0.4 * (
-            haw * ((s1p + s11 * af) + (s1q * df + s12 * ef))
-            + hdw * ((sqp + s1q * af) + (sqq * df + sq2 * ef))
-            + hew * ((s2p + s12 * af) + (sq2 * df + s22 * ef))
-        )
-    )
-    form.store(diag_ref, 0, 0.5 * (rain + total_2))
-    form.store(diag_ref, 1, (sum_y + 0.3 * sum_w) * (1.0 / (1.24 * CZ)))
-    form.store(diag_ref, 2, (sum_w - 0.8 * sum_y) * (1.0 / (1.24 * CZ)) - sb * (1.0 / CZ))
-
     mean_y = part_ref[pl.ds(0, CZ, stride=8), :]
     for s in range(1, 8):
         mean_y = mean_y + part_ref[pl.ds(s, CZ, stride=8), :]
     mean_y = form.join(mean_y) * (1.0 / CX)
-    hi, lo = halves(jnp.concatenate([mean_w, mean_y, jnp.zeros((ZP - CZ, LANES), F32)], 0))
-    return prof_ref[208:352, lanes] + dot(tail_ref[...], jnp.concatenate([hi, hi, lo], 0))
+    hi, lo = halves(jnp.concatenate([mean_y, jnp.zeros((ZP - CZ, LANES), F32)], 0))
+    tend = prof_ref[208:352, lanes] + dot(tail_ref[HALF:, :], jnp.concatenate([hi, hi, lo], 0))
+    sum_y = total_v - 0.62 * total_2
+    form.store(diag_ref, 0, 0.5 * (rain + total_2))
+    form.store(part_ref, 0, sum_y)
+    scale = 1.0 / (1.24 * CZ)
+    sums = part_ref[0:CX, :]
+    diag_ref[CX:2 * CX, :] = (diag_ref[CX:2 * CX, :] + sums) * scale
+    diag_ref[2 * CX:, :] = (diag_ref[2 * CX:, :] - 0.8 * sums) * scale
+    return tend
+
+
+def first_maps(maps_ref, ref, hi, lo):
+    ref[0:64, :] = dot(maps_ref[0:64, :], jnp.concatenate([hi[:80], hi[:80], lo[:80]], 0))
+    x = dot(maps_ref[64:208, :], jnp.concatenate([hi[80:160], hi[80:160], lo[80:160]], 0))
+    ref[64:128, :] = x[:64] + 0.5
+    ref[128:208, :] = x[64:]
+
+
+def more_maps(more_ref, ref, hi, lo):
+    ref[208:368, :] = dot(more_ref[...], jnp.concatenate([hi, hi, lo], 0))
 
 
 SENT = ((0, 80), (80, 72))
@@ -368,30 +388,22 @@
     loads[5].wait()
 
     def ordered(x):
+        pad = jnp.zeros((8, x.shape[1]), F32)
         return jnp.concatenate(
-            [x[LEV:2 * LEV] - 0.3 * x[0:LEV], x[2 * LEV:3 * LEV], x[0:LEV], x[3 * LEV:4 * LEV]], 0)
+            [x[LEV:2 * LEV] - 0.3 * x[0:LEV], pad, x[2 * LEV:3 * LEV], pad, x[0:LEV], x[3 * LEV:4 * LEV]], 0)
 
     hi, lo = halves(ordered(xs[...]))
-    hi_ref[0:288, :] = hi
-    lo_ref[0:288, :] = lo
+    hi_ref[0:304, :] = hi
+    lo_ref[0:304, :] = lo
     hi, lo = halves(su[...])
-    hi_ref[288:384, :] = hi
-    lo_ref[288:384, :] = lo
+    hi_ref[304:400, :] = hi
+    lo_ref[304:400, :] = lo
     for load in small[2:]:
         load.wait()
     pl.when(jnp.logical_and(e > 1, e < n_elem - 1))(exchange)
 
     def gather(ref, rows):
         return dot_t(ref[rows, :], ones_ref[...])
-
-    def first_maps(ref, hi, lo):
-        x = dot(maps_ref[...], jnp.concatenate([hi, hi, lo], 0))
-        ref[0:64, :] = x[:64]
-        ref[64:128, :] = x[64:128] + 0.5
-        ref[128:208, :] = x[128:]
-
-    def more_maps(ref, hi, lo):
-        ref[208:368, :] = dot(more_ref[...], jnp.concatenate([hi, hi, lo], 0))
 
     def to_next():
         for c in range(2):
@@ -407,9 +419,9 @@
     meanwhile = ({24: lambda: pl.when(e == 1)(exchange)}, {8: lambda: pl.when(first_e)(to_next)})
     main = slice(0, STATE_ROWS)
     hi, lo = gather(hi_ref, main).astype(BF16), gather(lo_ref, main).astype(BF16)
-    first_maps(prof, hi[:HALF], lo[:HALF])
-    more_maps(prof, hi, lo)
-    found = gather(hi_ref, slice(288, 384)) + gather(lo_ref, slice(288, 384))
+    first_maps(maps_ref, prof, hi, lo)
+    more_maps(more_ref, prof, jnp.concatenate([hi[:80], hi[160:]], 0), jnp.concatenate([lo[:80], lo[160:]], 0))
+    found = gather(hi_ref, slice(304, 400)) + gather(lo_ref, slice(304, 400))
     for i in range(2):
         lanes = tiles[i]
         sur[...] = found[:, lanes]
@@ -433,29 +445,33 @@
     out_ref[0:HALF, :] = xs[0:HALF, :] + back[0:HALF]
     diag_out_ref[...] = back[HALF:]
 
-    def edge(form, own_mass, on, wait, other_mass, arrived):
+    def edge(form, own_mass, on, wait, other_mass, arrived, emit):
         prep = prepare(form, sur)
         wait(0)
         masses = other_mass()
         scale = 1.0 / (own_mass + masses)
         share, rest = own_mass * scale, masses * scale
-        start = own_ref[0:HALF, :] * share + arrived(8) * rest
+        pad = jnp.zeros((8, LANES), F32)
+        py, p2 = arrived(8)
+        start = own_ref[0:160, :] * share + jnp.concatenate([py, pad, p2, pad], 0) * rest
         hi, lo = halves(start)
-        first_maps(edge_prof, hi, lo)
-        keep = []
+        first_maps(maps_ref, edge_prof, hi, lo)
+        both_p = []
 
         def late():
             wait(1)
-            final = own_ref[HALF:, :] * share + arrived(80) * rest
-            keep.append(final)
+            final = own_ref[160:, :] * share + jnp.concatenate(arrived(80), 0) * rest
             more_hi, more_lo = halves(final[:80])
-            more_maps(edge_prof, jnp.concatenate([hi, more_hi], 0), jnp.concatenate([lo, more_lo], 0))
+            more_maps(more_ref, edge_prof, jnp.concatenate([hi[:80], more_hi], 0),
+                      jnp.concatenate([lo[:80], more_lo], 0))
+            p0, p2, p3 = final[:LEV], start[80:152], final[LEV:]
+            both_p.append(jnp.concatenate([p0, start[:LEV] + 0.3 * p0], 0))
+            x = jnp.concatenate([p2, p3], 0)
+            emit(slice(HALF, 2 * HALF), x + jnp.where(on, passive(x, sur[2 * CX:, :]), 0.0))
 
         tend = cloud(form, consts, prep, edge_prof, tiles[0], tail_ref, lev_ref, part, diag, {24: late})
-        py, p2, p0, p3 = start[:LEV], start[LEV:], keep[0][:LEV], keep[0][LEV:]
-        slow = passive(jnp.concatenate([p2, p3], 0), sur[2 * CX:, :])
-        shared = jnp.concatenate([p0, py + 0.3 * p0, p2, p3], 0)
-        return shared + jnp.where(on, jnp.concatenate([tend, slow], 0), 0.0), jnp.where(on, diag[...], 0.0)
+        emit(slice(0, HALF), both_p[0] + jnp.where(on, tend, 0.0))
+        return jnp.where(on, diag[...], 0.0)
 
     def one_end(k, _):
         i, got = k, 1 - k
@@ -468,15 +484,17 @@
         def arrived(row):
             x = recv[got, row:row + LEV, :]
             y = swap(x)
-            return jnp.concatenate([jnp.where(low, x, y), jnp.where(low, y, x)], 0)
+            return jnp.where(low, x, y), jnp.where(low, y, x)
+
+        def emit(rows, new):
+            out_ref[rows, lanes] = jnp.where(side, new, out_ref[rows, lanes])
 
         sur[...] = double(su[:, lanes])
         own_ref[...] = ordered(double(xs[:, lanes]))
-        new, seen = edge(
+        seen = edge(
             Half, double(mass_ref[:, lanes]), jnp.where(side, active_ref[:, lanes], 0) == 1,
             lambda c: pl.when(jnp.logical_not(jnp.logical_and(first_e, got == 1)))(end_copy(c, got).wait_recv),
-            lambda: recv[got, 0:1, :], arrived)
-        out_ref[:, lanes] = jnp.where(side, new, out_ref[:, lanes])
+            lambda: recv[got, 0:1, :], arrived, emit)
         diag_out_ref[:, lanes] = jnp.where(side, seen, diag_out_ref[:, lanes])
         return 0
 
@@ -492,15 +510,17 @@
 
         def arrived(row):
             x, y = recv[0, row:row + LEV, :], recv[1, row:row + LEV, :]
-            return jnp.concatenate([jnp.where(low, x, swap(y)), jnp.where(low, swap(x), y)], 0)
+            return jnp.where(low, x, swap(y)), jnp.where(low, swap(x), y)
+
+        def emit(rows, new):
+            out_ref[rows, t0] = jnp.where(low, new, out_ref[rows, t0])
+            out_ref[rows, t3] = jnp.where(low, out_ref[rows, t3], new)
 
         sur[...] = merge(su)
         own_ref[...] = ordered(merge(xs))
-        new, seen = edge(
+        seen = edge(
             Whole, merge(mass_ref), merge(active_ref) == 1, wait,
-            lambda: jnp.where(low, recv[0, 0:1, :], recv[1, 0:1, :]), arrived)
-        out_ref[:, t0] = jnp.where(low, new, out_ref[:, t0])
-        out_ref[:, t3] = jnp.where(low, out_ref[:, t3], new)
+            lambda: jnp.where(low, recv[0, 0:1, :], recv[1, 0:1, :]), arrived, emit)
         diag_out_ref[:, t0] = jnp.where(low, seen, diag_out_ref[:, t0])
         diag_out_ref[:, t3] = jnp.where(low, diag_out_ref[:, t3], seen)
 
@@ -541,8 +561,8 @@
         out_specs=(vmem, vmem),
         scratch_shapes=[
             pltpu.VMEM((4 * LEV, cols), F32),
-            pltpu.VMEM((384, cols), BF16),
-            pltpu.VMEM((384, cols), BF16),
+            pltpu.VMEM((400, cols), BF16),
+            pltpu.VMEM((400, cols), BF16),
             pltpu.VMEM((3 * CX, cols), F32),
             pltpu.VMEM((2 * BLOCK, cols), BF16),
             pltpu.VMEM((2, HALF + 8, LANES), F32),
@@ -554,7 +574,7 @@
             pltpu.VMEM((3 * CX, BLOCK), F32),
             pltpu.VMEM((HALF + 3 * CX, 2 * BLOCK), BF16),
             pltpu.VMEM((HALF + 3 * CX, 2 * BLOCK), BF16),
-            pltpu.VMEM((4 * LEV, LANES), F32),
+            pltpu.VMEM((4 * LEV + 16, LANES), F32),
             pltpu.VMEM((1, cols), F32),
             pltpu.VMEM((1, cols), jnp.int32),
             pltpu.VMEM(maps.shape, BF16),

time: 11.9 us -> 11.9 us (level)
  no operation moved by 1% of the time
where the time goes in v4:
time: 11.9 us; the launch traced here: 11.8 us
  Pallas kernels  11.1 us (93%)
  between operations  0.64 us (5%)
    pallas_call x1, Pallas kernels, body(): pl.pallas_call(functools.partial(kernel, consts, n_elem), out_shape=(pltp...  10.2 us
    pallas_call x1, Pallas kernels, body(): pl.pallas_call(write, out_shape=(jax.ShapeDtypeStruct(new_state.shape, F3...  0.89 us

profile of v4, /device:TPU:0, one launch (start us, length us, event | category | flops | bytes accessed | tf_op | source)
XLA Modules:
  0.0 11.8 jit_solution(50294195837482634)
XLA Ops:
  0.6 10.2 %shard_map.113 = (f32[288,512]{1,0:T(8,128)S(1)}, f32[96,512]{1,0:T(8,128)S(1)}) custom-call(f32[288,512]{1,0:T(8,128)} %bitcast.6, f32[96,512]{1,0:T(8,128)} %bitcast.7, f32[1,512]{1,0:T(1,128)} %bitcast.8, s32[1,512]{1,0:T(1,128)} %bitcast.9, bf16[208,240]{1,0:T(8,128)(2,1)} %constant.12.clone.maps_hbm, bf16[160,480]{1,0:T(8,128)(2,1)} %constant.13.clone.more_hbm, ...), custom_call_target="tpu_custom_call" | custom-call | tf_op jit(solution)/shard_map/pallas_call | solution.py:557
  10.9 0.9 %shard_map.114 = (f32[288,512]{1,0:T(8,128)}, f32[96,512]{1,0:T(8,128)}) custom-call(f32[288,512]{1,0:T(8,128)S(1)} %get-tuple-element.6.state_ref, f32[96,512]{1,0:T(8,128)S(1)} %get-tuple-element.7.diag_ref), custom_call_target="tpu_custom_call" | custom-call | tf_op jit(solution)/shard_map/pallas_call | solution.py:595

commit v5 on v4

--- a/solution.py
+++ b/solution.py
@@ -205,7 +205,7 @@
     return s2, ay, dy, af, df, aw, dw, ef, haw, hdw, hew, gram, means
 
 
-def cloud(form, consts, prep, prof_ref, lanes, tail_ref, lev_ref, part_ref, diag_ref, at={}):
+def cloud(form, consts, prep, prof_ref, lanes, tail_ref, lev_ref, part_ref, diag_ref, at={}, steady=None):
     s2, ay, dy, af, df, aw, dw, ef, haw, hdw, hew, gram, means = prep
     east, west = form.east, form.west
 
@@ -213,9 +213,14 @@
         return prof_ref[start + z:start + z + 1, lanes][None]
 
     def horizontal(z):
-        turn = level(128, z) + consts["c2"][z] * s2
-        y = (level(0, z) + consts["c1"][z] * ay) + turn * dy
-        pull = (level(64, z) + consts["c1"][z] * af) + turn * df
+        if steady is None:
+            turn = level(128, z) + consts["c2"][z] * s2
+            y = (level(0, z) + consts["c1"][z] * ay) + turn * dy
+            pull = (level(64, z) + consts["c1"][z] * af) + turn * df
+        else:
+            turn = level(128, z)
+            y = (level(0, z) + steady[z, 0]) + turn * dy
+            pull = (level(64, z) + steady[z, 1]) + turn * df
         one = jnp.log(1.0 + jnp.exp2(y * (0.62 * math.log2(math.e))))
         y = y - one
         e, w = east(y), west(y)
@@ -304,7 +309,7 @@
 
 def kernel(consts, n_elem, state_ref, surface_ref, mass_hbm, active_hbm, maps_hbm, more_hbm, tail_hbm, passive_hbm,
            drift_hbm, lev_hbm, out_ref, diag_out_ref,
-           xs, hi_ref, lo_ref, su, ones_ref, send, recv, sur, prof, edge_prof, part, diag, both_hi, both_lo, own_ref,
+           xs, hi_ref, lo_ref, su, ones_ref, send, recv, sur, prof, edge_prof, part, diag, both_hi, both_lo, own_ref, steady_ref,
            mass_ref, active_ref, maps_ref, more_ref, tail_ref, passive_ref, drift_ref, lev_ref,
            in_sem, send_sem, recv_sem):
     e, g = lax.axis_index("elem"), lax.axis_index("grp")
@@ -447,6 +452,14 @@
 
     def edge(form, own_mass, on, wait, other_mass, arrived, emit):
         prep = prepare(form, sur)
+        steady = None
+        if form is Half:
+            steady = steady_ref
+            s2, ay, dy, af, df = prep[:5]
+            sdy, sdf = s2 * dy, s2 * df
+            for z in range(CZ):
+                steady[z, 0] = consts["c1"][z] * ay + consts["c2"][z] * sdy
+                steady[z, 1] = consts["c1"][z] * af + consts["c2"][z] * sdf
         wait(0)
         masses = other_mass()
         scale = 1.0 / (own_mass + masses)
@@ -469,7 +482,7 @@
             x = jnp.concatenate([p2, p3], 0)
             emit(slice(HALF, 2 * HALF), x + jnp.where(on, passive(x, sur[2 * CX:, :]), 0.0))
 
-        tend = cloud(form, consts, prep, edge_prof, tiles[0], tail_ref, lev_ref, part, diag, {24: late})
+        tend = cloud(form, consts, prep, edge_prof, tiles[0], tail_ref, lev_ref, part, diag, {24: late}, steady)
         emit(slice(0, HALF), both_p[0] + jnp.where(on, tend, 0.0))
         return jnp.where(on, diag[...], 0.0)
 
@@ -575,6 +588,7 @@
             pltpu.VMEM((HALF + 3 * CX, 2 * BLOCK), BF16),
             pltpu.VMEM((HALF + 3 * CX, 2 * BLOCK), BF16),
             pltpu.VMEM((4 * LEV + 16, LANES), F32),
+            pltpu.VMEM((CZ, 2, 2, 8, LANES), F32),
             pltpu.VMEM((1, cols), F32),
             pltpu.VMEM((1, cols), jnp.int32),
             pltpu.VMEM(maps.shape, BF16),

time: 11.9 us -> 11.8 us (level)
  no operation moved by 1% of the time
where the time goes in v5:
time: 11.8 us; the launch traced here: 11.7 us
  Pallas kernels  11 us (93%)
  between operations  0.64 us (5%)
    pallas_call x1, Pallas kernels, body(): pl.pallas_call(functools.partial(kernel, consts, n_elem), out_shape=(pltp...  10.2 us
    pallas_call x1, Pallas kernels, body(): pl.pallas_call(write, out_shape=(jax.ShapeDtypeStruct(new_state.shape, F3...  0.89 us

profile of v5, /device:TPU:0, one launch (start us, length us, event | category | flops | bytes accessed | tf_op | source)
XLA Modules:
  0.0 11.7 jit_solution(8554669692537490888)
XLA Ops:
  0.6 10.2 %shard_map.113 = (f32[288,512]{1,0:T(8,128)S(1)}, f32[96,512]{1,0:T(8,128)S(1)}) custom-call(f32[288,512]{1,0:T(8,128)} %bitcast.6, f32[96,512]{1,0:T(8,128)} %bitcast.7, f32[1,512]{1,0:T(1,128)} %bitcast.8, s32[1,512]{1,0:T(1,128)} %bitcast.9, bf16[208,240]{1,0:T(8,128)(2,1)} %constant.12.clone.maps_hbm, bf16[160,480]{1,0:T(8,128)(2,1)} %constant.13.clone.more_hbm, ...), custom_call_target="tpu_custom_call" | custom-call | tf_op jit(solution)/shard_map/pallas_call | solution.py:570
  10.8 0.9 %shard_map.114 = (f32[288,512]{1,0:T(8,128)}, f32[96,512]{1,0:T(8,128)}) custom-call(f32[288,512]{1,0:T(8,128)S(1)} %get-tuple-element.6.state_ref, f32[96,512]{1,0:T(8,128)S(1)} %get-tuple-element.7.diag_ref), custom_call_target="tpu_custom_call" | custom-call | tf_op jit(solution)/shard_map/pallas_call | solution.py:609

commit v6 on v5

--- a/solution.py
+++ b/solution.py
@@ -264,7 +264,7 @@
     for z in range(CZ):
         if z in at:
             at[z]()
-        if z == 26:
+        if z == 36:
             sum_w = passive_sums()
             form.store(diag_ref, 1, 0.3 * sum_w)
             form.store(diag_ref, 2, sum_w - 1.24 * prof_ref[353:354, lanes])
@@ -304,7 +304,7 @@
     ref[208:368, :] = dot(more_ref[...], jnp.concatenate([hi, hi, lo], 0))
 
 
-SENT = ((0, 80), (80, 72))
+SENT = ((0, 48), (48, 40), (88, 72))
 
 
 def kernel(consts, n_elem, state_ref, surface_ref, mass_hbm, active_hbm, maps_hbm, more_hbm, tail_hbm, passive_hbm,
@@ -324,10 +324,10 @@
     loads = [
         pltpu.make_async_copy(state_ref.at[rows, lanes], xs.at[rows, lanes], in_sem.at[k])
         for k, (rows, lanes) in enumerate(
-            (rows, lanes) for rows in (slice(0, 3 * LEV), slice(3 * LEV, 4 * LEV)) for lanes in ends)
+            (rows, lanes) for rows in (slice(2 * LEV, 3 * LEV), slice(0, 2 * LEV), slice(3 * LEV, 4 * LEV)) for lanes in ends)
     ] + [
-        pltpu.make_async_copy(state_ref.at[:, pl.ds(LANES, 2 * LANES)], xs.at[:, pl.ds(LANES, 2 * LANES)], in_sem.at[4]),
-        pltpu.make_async_copy(surface_ref, su, in_sem.at[5]),
+        pltpu.make_async_copy(state_ref.at[:, pl.ds(LANES, 2 * LANES)], xs.at[:, pl.ds(LANES, 2 * LANES)], in_sem.at[14]),
+        pltpu.make_async_copy(surface_ref, su, in_sem.at[15]),
     ]
     small = [
         pltpu.make_async_copy(a, b, in_sem.at[6 + i])
@@ -335,7 +335,7 @@
             (mass_hbm, mass_ref), (active_hbm, active_ref), (maps_hbm, maps_ref), (lev_hbm, lev_ref),
             (more_hbm, more_ref), (tail_hbm, tail_ref), (passive_hbm, passive_ref), (drift_hbm, drift_ref)))
     ]
-    for load in small[:1] + loads[:4] + small[1:2] + loads[4:] + small[2:]:
+    for load in loads[:1] + small[:1] + loads[2:3] + loads[1:2] + loads[3:6] + small[1:2] + loads[6:] + small[2:]:
         load.start()
 
     low = lax.broadcasted_iota(jnp.int32, (1, LANES), 1) < EDGE
@@ -347,7 +347,7 @@
             send_sem=send_sem.at[2 * c + i], recv_sem=recv_sem.at[2 * c + i],
             device_id=((after, before)[i] if isinstance(i, int) else after, g), device_id_type=MESH)
 
-    sent = [end_copy(c, i) for i in range(2) for c in range(2)]
+    sent = [end_copy(c, i) for i in range(2) for c in range(3)]
 
     def enter():
         pl.semaphore_wait(barrier, 2)
@@ -364,15 +364,22 @@
         mass = mass_ref[:, lanes]
         mass = jnp.where(low, swap(mass), mass) if i == 0 else jnp.where(low, mass, swap(mass))
         send[i, 0:8, :] = jnp.broadcast_to(mass, (8, LANES))
+
+        def folded(x):
+            top, bottom = x[:40], jnp.concatenate([x[40:], jnp.zeros((8, LANES), F32)], 0)
+            return jnp.where(low, swap(top), bottom) if i == 0 else jnp.where(low, top, swap(bottom))
+
         loads[i].wait()
+        send[i, 8:48, :] = folded(xs[2 * LEV:3 * LEV, lanes])
+        pl.when(last_e)(sent[3 * i].start)
+        loads[2 + i].wait()
         p0 = xs[0:LEV, lanes]
-        py, p2 = xs[LEV:2 * LEV, lanes] - 0.3 * p0, xs[2 * LEV:3 * LEV, lanes]
-        send[i, 8:80, :] = jnp.where(low, swap(py), p2) if i == 0 else jnp.where(low, py, swap(p2))
-        pl.when(last_e)(sent[2 * i].start)
-        loads[2 + i].wait()
-        p0, p3 = xs[0:LEV, lanes], xs[3 * LEV:, lanes]
-        send[i, 80:152, :] = jnp.where(low, swap(p0), p3) if i == 0 else jnp.where(low, p0, swap(p3))
-        pl.when(last_e)(sent[2 * i + 1].start)
+        send[i, 48:88, :] = folded(xs[LEV:2 * LEV, lanes] - 0.3 * p0)
+        pl.when(last_e)(sent[3 * i + 1].start)
+        loads[4 + i].wait()
+        p3 = xs[3 * LEV:, lanes]
+        send[i, 88:160, :] = jnp.where(low, swap(p0), p3) if i == 0 else jnp.where(low, p0, swap(p3))
+        pl.when(last_e)(sent[3 * i + 2].start)
 
     small[1].wait()
     act = [active_ref[:, lanes].astype(F32) for lanes in tiles]
@@ -389,8 +396,8 @@
         ones_ref[:, lanes] = jnp.where(where == place, 1.0, 0.0).astype(BF16)
         offset = offset + counts[b:b + 1, LANES:]
 
-    loads[4].wait()
-    loads[5].wait()
+    loads[6].wait()
+    loads[7].wait()
 
     def ordered(x):
         pad = jnp.zeros((8, x.shape[1]), F32)
@@ -411,15 +418,15 @@
         return dot_t(ref[rows, :], ones_ref[...])
 
     def to_next():
-        for c in range(2):
+        for c in range(3):
             end_copy(c, 1).wait_recv()
-        sent[0].start()
-        sent[1].start()
+        for copy in sent[:3]:
+            copy.start()
 
     def to_previous():
         enter()
-        sent[2].start()
-        sent[3].start()
+        for copy in sent[3:]:
+            copy.start()
 
     meanwhile = ({24: lambda: pl.when(e == 1)(exchange)}, {8: lambda: pl.when(first_e)(to_next)})
     main = slice(0, STATE_ROWS)
@@ -461,19 +468,20 @@
                 steady[z, 0] = consts["c1"][z] * ay + consts["c2"][z] * sdy
                 steady[z, 1] = consts["c1"][z] * af + consts["c2"][z] * sdf
         wait(0)
+        wait(1)
         masses = other_mass()
         scale = 1.0 / (own_mass + masses)
         share, rest = own_mass * scale, masses * scale
         pad = jnp.zeros((8, LANES), F32)
-        py, p2 = arrived(8)
+        p2, py = [jnp.concatenate([a, b[:32]], 0) for a, b in (arrived(8, 40), arrived(48, 40))]
         start = own_ref[0:160, :] * share + jnp.concatenate([py, pad, p2, pad], 0) * rest
         hi, lo = halves(start)
         first_maps(maps_ref, edge_prof, hi, lo)
         both_p = []
 
         def late():
-            wait(1)
-            final = own_ref[160:, :] * share + jnp.concatenate(arrived(80), 0) * rest
+            wait(2)
+            final = own_ref[160:, :] * share + jnp.concatenate(arrived(88, LEV), 0) * rest
             more_hi, more_lo = halves(final[:80])
             more_maps(more_ref, edge_prof, jnp.concatenate([hi[:80], more_hi], 0),
                       jnp.concatenate([lo[:80], more_lo], 0))
@@ -482,7 +490,7 @@
             x = jnp.concatenate([p2, p3], 0)
             emit(slice(HALF, 2 * HALF), x + jnp.where(on, passive(x, sur[2 * CX:, :]), 0.0))
 
-        tend = cloud(form, consts, prep, edge_prof, tiles[0], tail_ref, lev_ref, part, diag, {24: late}, steady)
+        tend = cloud(form, consts, prep, edge_prof, tiles[0], tail_ref, lev_ref, part, diag, {34: late}, steady)
         emit(slice(0, HALF), both_p[0] + jnp.where(on, tend, 0.0))
         return jnp.where(on, diag[...], 0.0)
 
@@ -494,8 +502,8 @@
         def double(x):
             return jnp.where(side, x, swap(x))
 
-        def arrived(row):
-            x = recv[got, row:row + LEV, :]
+        def arrived(row, count):
+            x = recv[got, row:row + count, :]
             y = swap(x)
             return jnp.where(low, x, y), jnp.where(low, y, x)
 
@@ -521,8 +529,8 @@
             for got in range(2):
                 end_copy(c, got).wait_recv()
 
-        def arrived(row):
-            x, y = recv[0, row:row + LEV, :], recv[1, row:row + LEV, :]
+        def arrived(row, count):
+            x, y = recv[0, row:row + count, :], recv[1, row:row + count, :]
             return jnp.where(low, x, swap(y)), jnp.where(low, swap(x), y)
 
         def emit(rows, new):
@@ -578,8 +586,8 @@
             pltpu.VMEM((400, cols), BF16),
             pltpu.VMEM((3 * CX, cols), F32),
             pltpu.VMEM((2 * BLOCK, cols), BF16),
-            pltpu.VMEM((2, HALF + 8, LANES), F32),
-            pltpu.VMEM((2, HALF + 8, LANES), F32),
+            pltpu.VMEM((2, 160, LANES), F32),
+            pltpu.VMEM((2, 160, LANES), F32),
             pltpu.VMEM((3 * CX, BLOCK), F32),
             pltpu.VMEM((368, 2 * BLOCK), F32),
             pltpu.VMEM((368, BLOCK), F32),
@@ -597,9 +605,9 @@
             pltpu.VMEM(passive.shape, BF16),
             pltpu.VMEM(drift.shape, F32),
             pltpu.VMEM(levels.shape, F32),
-            pltpu.SemaphoreType.DMA((14,)),
-            pltpu.SemaphoreType.DMA((4,)),
-            pltpu.SemaphoreType.DMA((4,)),
+            pltpu.SemaphoreType.DMA((16,)),
+            pltpu.SemaphoreType.DMA((6,)),
+            pltpu.SemaphoreType.DMA((6,)),
         ],
         compiler_params=pltpu.CompilerParams(
             collective_id=0, has_side_effects=True, vmem_limit_bytes=32 * 1024 * 1024),

time: 11.8 us -> 11.8 us (level)
  no operation moved by 1% of the time
where the time goes in v6:
time: 11.8 us; the launch traced here: 11.6 us
  Pallas kernels  11 us (93%)
  between operations  0.64 us (5%)
    pallas_call x1, Pallas kernels, body(): pl.pallas_call(functools.partial(kernel, consts, n_elem), out_shape=(pltp...  10.1 us
    pallas_call x1, Pallas kernels, body(): pl.pallas_call(write, out_shape=(jax.ShapeDtypeStruct(new_state.shape, F3...  0.89 us

profile of v6, /device:TPU:0, one launch (start us, length us, event | category | flops | bytes accessed | tf_op | source)
XLA Modules:
  0.0 11.6 jit_solution(15228617479388309518)
XLA Ops:
  0.6 10.1 %shard_map.113 = (f32[288,512]{1,0:T(8,128)S(1)}, f32[96,512]{1,0:T(8,128)S(1)}) custom-call(f32[288,512]{1,0:T(8,128)} %bitcast.6, f32[96,512]{1,0:T(8,128)} %bitcast.7, f32[1,512]{1,0:T(1,128)} %bitcast.8, s32[1,512]{1,0:T(1,128)} %bitcast.9, bf16[208,240]{1,0:T(8,128)(2,1)} %constant.12.clone.maps_hbm, bf16[160,480]{1,0:T(8,128)(2,1)} %constant.13.clone.more_hbm, ...), custom_call_target="tpu_custom_call" | custom-call | tf_op jit(solution)/shard_map/pallas_call | solution.py:578
  10.7 0.9 %shard_map.114 = (f32[288,512]{1,0:T(8,128)}, f32[96,512]{1,0:T(8,128)}) custom-call(f32[288,512]{1,0:T(8,128)S(1)} %get-tuple-element.6.state_ref, f32[96,512]{1,0:T(8,128)S(1)} %get-tuple-element.7.diag_ref), custom_call_target="tpu_custom_call" | custom-call | tf_op jit(solution)/shard_map/pallas_call | solution.py:617

commit v7 on v6

--- a/solution.py
+++ b/solution.py
@@ -293,9 +293,12 @@
     return tend
 
 
-def first_maps(maps_ref, ref, hi, lo):
-    ref[0:64, :] = dot(maps_ref[0:64, :], jnp.concatenate([hi[:80], hi[:80], lo[:80]], 0))
-    x = dot(maps_ref[64:208, :], jnp.concatenate([hi[80:160], hi[80:160], lo[80:160]], 0))
+def maps_1(maps_ref, ref, hi, lo):
+    ref[0:64, :] = dot(maps_ref[0:64, :], jnp.concatenate([hi, hi, lo], 0))
+
+
+def maps_2(maps_ref, ref, hi, lo):
+    x = dot(maps_ref[64:208, :], jnp.concatenate([hi, hi, lo], 0))
     ref[64:128, :] = x[:64] + 0.5
     ref[128:208, :] = x[64:]
 
@@ -431,7 +434,8 @@
     meanwhile = ({24: lambda: pl.when(e == 1)(exchange)}, {8: lambda: pl.when(first_e)(to_next)})
     main = slice(0, STATE_ROWS)
     hi, lo = gather(hi_ref, main).astype(BF16), gather(lo_ref, main).astype(BF16)
-    first_maps(maps_ref, prof, hi, lo)
+    maps_1(maps_ref, prof, hi[:80], lo[:80])
+    maps_2(maps_ref, prof, hi[80:160], lo[80:160])
     more_maps(more_ref, prof, jnp.concatenate([hi[:80], hi[160:]], 0), jnp.concatenate([lo[:80], lo[160:]], 0))
     found = gather(hi_ref, slice(304, 400)) + gather(lo_ref, slice(304, 400))
     for i in range(2):
@@ -468,25 +472,32 @@
                 steady[z, 0] = consts["c1"][z] * ay + consts["c2"][z] * sdy
                 steady[z, 1] = consts["c1"][z] * af + consts["c2"][z] * sdf
         wait(0)
-        wait(1)
         masses = other_mass()
         scale = 1.0 / (own_mass + masses)
         share, rest = own_mass * scale, masses * scale
         pad = jnp.zeros((8, LANES), F32)
-        p2, py = [jnp.concatenate([a, b[:32]], 0) for a, b in (arrived(8, 40), arrived(48, 40))]
-        start = own_ref[0:160, :] * share + jnp.concatenate([py, pad, p2, pad], 0) * rest
-        hi, lo = halves(start)
-        first_maps(maps_ref, edge_prof, hi, lo)
+
+        def shared(row, at):
+            top, bottom = arrived(row, 40)
+            x = jnp.concatenate([top, bottom[:32], pad], 0)
+            return own_ref[at:at + 80, :] * share + x * rest
+
+        second = shared(8, 80)
+        maps_2(maps_ref, edge_prof, *halves(second))
+        wait(1)
+        first = shared(48, 0)
+        hi, lo = halves(first)
+        maps_1(maps_ref, edge_prof, hi, lo)
         both_p = []
 
         def late():
             wait(2)
             final = own_ref[160:, :] * share + jnp.concatenate(arrived(88, LEV), 0) * rest
             more_hi, more_lo = halves(final[:80])
-            more_maps(more_ref, edge_prof, jnp.concatenate([hi[:80], more_hi], 0),
-                      jnp.concatenate([lo[:80], more_lo], 0))
-            p0, p2, p3 = final[:LEV], start[80:152], final[LEV:]
-            both_p.append(jnp.concatenate([p0, start[:LEV] + 0.3 * p0], 0))
+            more_maps(more_ref, edge_prof, jnp.concatenate([hi, more_hi], 0),
+                      jnp.concatenate([lo, more_lo], 0))
+            p0, p2, p3 = final[:LEV], second[:LEV], final[LEV:]
+            both_p.append(jnp.concatenate([p0, first[:LEV] + 0.3 * p0], 0))
             x = jnp.concatenate([p2, p3], 0)
             emit(slice(HALF, 2 * HALF), x + jnp.where(on, passive(x, sur[2 * CX:, :]), 0.0))
 

time: 11.8 us -> 12 us (1.017)
  Pallas kernels: 11 us -> 11.3 us
    pallas_call x1, Pallas kernels: 10.1 us -> 10.4 us  [body(): pl.pallas_call(functools.partial(kernel, consts, n_elem), out_shape=(pltp...]
where the time goes in v7:
time: 12 us; the launch traced here: 11.9 us
  Pallas kernels  11.3 us (94%)
  between operations  0.64 us (5%)
    pallas_call x1, Pallas kernels, body(): pl.pallas_call(functools.partial(kernel, consts, n_elem), out_shape=(pltp...  10.4 us
    pallas_call x1, Pallas kernels, body(): pl.pallas_call(write, out_shape=(jax.ShapeDtypeStruct(new_state.shape, F3...  0.89 us

profile of v7, /device:TPU:0, one launch (start us, length us, event | category | flops | bytes accessed | tf_op | source)
XLA Modules:
  0.0 11.9 jit_solution(11230132127313842304)
XLA Ops:
  0.6 10.4 %shard_map.113 = (f32[288,512]{1,0:T(8,128)S(1)}, f32[96,512]{1,0:T(8,128)S(1)}) custom-call(f32[288,512]{1,0:T(8,128)} %bitcast.6, f32[96,512]{1,0:T(8,128)} %bitcast.7, f32[1,512]{1,0:T(1,128)} %bitcast.8, s32[1,512]{1,0:T(1,128)} %bitcast.9, bf16[208,240]{1,0:T(8,128)(2,1)} %constant.12.clone.maps_hbm, bf16[160,480]{1,0:T(8,128)(2,1)} %constant.13.clone.more_hbm, ...), custom_call_target="tpu_custom_call" | custom-call | tf_op jit(solution)/shard_map/pallas_call | solution.py:589
  11.0 0.9 %shard_map.114 = (f32[288,512]{1,0:T(8,128)}, f32[96,512]{1,0:T(8,128)}) custom-call(f32[288,512]{1,0:T(8,128)S(1)} %get-tuple-element.6.state_ref, f32[96,512]{1,0:T(8,128)S(1)} %get-tuple-element.7.diag_ref), custom_call_target="tpu_custom_call" | custom-call | tf_op jit(solution)/shard_map/pallas_call | solution.py:628
